TPU v7x, 32 devices: a whole 2x2x4 slice. The times are simulated.
32 devices in a mesh: ctx: 8 (over y, x, core), fsdp: 4 (over z).
Axes of the slice: x: 2, y: 2, z: 4, core: 2. Of those that a mesh axis runs over, the one named last changes fastest.
Arguments:
- tokens: bfloat16 [4, 1024, 768], P('fsdp', 'ctx'), may hold values from -6 to 6
- encoder: bfloat16 [4, 512, 768], P('fsdp', 'ctx'), may hold values from -6 to 6
- cotangent: bfloat16 [4, 1024, 768], P('fsdp', 'ctx'), may hold values from -6 to 6
- buckets: int32 [1024], replicated, may hold values from 0 to 31
- pairing: int32 [8], replicated, may hold values from 0 to 7, each once
- norm_one: bfloat16 [768], P('fsdp'), may hold values from 0.5 to 1.5
- self_query: bfloat16 [768, 768], P('fsdp'), may hold values from -0.02734375 to 0.02734375
- self_key: bfloat16 [768, 768], P('fsdp'), may hold values from -0.21875 to 0.21875
- self_value: bfloat16 [768, 768], P('fsdp'), may hold values from -0.21875 to 0.21875
- self_output: bfloat16 [768, 768], P('fsdp'), may hold values from -1.25 to 1.25
- bias_table: bfloat16 [32, 12], P('fsdp'), may hold values from -4 to 4
- norm_two: bfloat16 [768], P('fsdp'), may hold values from 0.5 to 1.5
- cross_query: bfloat16 [768, 768], P('fsdp'), may hold values from -0.02734375 to 0.02734375
- cross_key: bfloat16 [768, 768], P('fsdp'), may hold values from -0.21875 to 0.21875
- cross_value: bfloat16 [768, 768], P('fsdp'), may hold values from -0.21875 to 0.21875
- cross_output: bfloat16 [768, 768], P('fsdp'), may hold values from -1.75 to 1.75
- norm_three: bfloat16 [768], P('fsdp'), may hold values from 0.5 to 1.5
- ff_gate: bfloat16 [768, 2048], P('fsdp'), may hold values from -0.21875 to 0.21875
- ff_up: bfloat16 [768, 2048], P('fsdp'), may hold values from -0.21875 to 0.21875
- ff_down: bfloat16 [2048, 768], P('fsdp'), may hold values from -0.125 to 0.125
Outputs:
- output: bfloat16 [4, 1024, 768], P('fsdp', 'ctx')
- grad_tokens: float32 [4, 1024, 768], P('fsdp', 'ctx')
- grad_encoder: float32 [4, 512, 768], P('fsdp', 'ctx')
- grad_norm_one: float32 [768], P('fsdp')
- grad_self_query: float32 [768, 768], P('fsdp')
- grad_self_key: float32 [768, 768], P('fsdp')
- grad_self_value: float32 [768, 768], P('fsdp')
- grad_self_output: float32 [768, 768], P('fsdp')
- grad_bias_table: float32 [32, 12], P('fsdp')
- grad_norm_two: float32 [768], P('fsdp')
- grad_cross_query: float32 [768, 768], P('fsdp')
- grad_cross_key: float32 [768, 768], P('fsdp')
- grad_cross_value: float32 [768, 768], P('fsdp')
- grad_cross_output: float32 [768, 768], P('fsdp')
- grad_norm_three: float32 [768], P('fsdp')
- grad_ff_gate: float32 [768, 2048], P('fsdp')
- grad_ff_up: float32 [768, 2048], P('fsdp')
- grad_ff_down: float32 [2048, 768], P('fsdp')
All inputs are finite; a program needn't handle non-finite values.
Results may differ from a plain program's by a relative error of at most 0.03.
Values may be sent and summed in bfloat16 or wider, within the bound.
No kernel may reach another device: no remote copies, remote signals or barrier semaphores. Data moves between devices by JAX's collectives and lax.ppermute only.
A program may use at most 192 MiB of HBM per device.

v0:
```python
import jax
import jax.numpy as jnp
from jax import lax
from jax.sharding import PartitionSpec as P


def norm_apply(v, g):
    return v * lax.rsqrt(jnp.mean(v * v, axis=-1, keepdims=True) + 1e-06) * g


def product(a, w):
    return jnp.dot(a, w, preferred_element_type=jnp.float32)


def through(grad, w):
    return jnp.einsum("tf,df->td", grad, w, preferred_element_type=jnp.float32)


def weight_grad(a, grad):
    return jnp.einsum("td,tf->df", a, grad, preferred_element_type=jnp.float32)


def split_heads(v, heads):
    return v.reshape(v.shape[0], heads, -1)


def pair_buckets(buckets, query_pos, key_pos, seq_len, nbuckets):
    distance = query_pos[:, None] - key_pos[None, :]
    keep = distance >= 0
    spots = jnp.clip(distance, 0, seq_len - 1)
    bucket_ids = jnp.take(buckets, spots)
    matches = bucket_ids[:, :, None] == jnp.arange(nbuckets, dtype=jnp.int32)[None, None, :]
    onehot = jnp.logical_and(matches, keep[:, :, None]).astype(jnp.bfloat16)
    return (onehot, keep)


def pair_bias(onehot, relative_bias_table):
    return jnp.einsum(
        "qkc,ch->hqk", onehot, relative_bias_table, preferred_element_type=jnp.float32
    )


def table_gradient(score_gradient, onehot):
    return jnp.einsum("hqk,qkc->ch", score_gradient, onehot, preferred_element_type=jnp.float32)


def score_rows(queries, keys, heads, extra, keep):
    scores = jnp.einsum(
        "qhd,khd->hqk",
        split_heads(queries, heads),
        split_heads(keys, heads),
        preferred_element_type=jnp.float32,
    )
    if extra is None:
        return scores
    return jnp.where(keep[None], scores + extra, -1e30)


def attend(queries, keys, values, heads, extra, keep):
    scores = score_rows(queries, keys, heads, extra, keep)
    top = jnp.max(scores, axis=-1, keepdims=True)
    expo = jnp.exp(scores - top)
    total = jnp.sum(expo, axis=-1, keepdims=True)
    probs = (expo / total).astype(jnp.bfloat16)
    result = jnp.einsum(
        "hqk,khd->qhd", probs, split_heads(values, heads), preferred_element_type=jnp.float32
    )
    return (result.reshape(queries.shape[0], -1), top + jnp.log(total))


def score_grads(queries, keys, values, heads, extra, keep, lse, grad_out, delta):
    scores = score_rows(queries, keys, heads, extra, keep)
    probs = jnp.exp(scores - lse)
    dprob = jnp.einsum(
        "qhd,khd->hqk",
        split_heads(grad_out, heads),
        split_heads(values, heads),
        preferred_element_type=jnp.float32,
    )
    delta = jnp.sum(probs * dprob, axis=-1, keepdims=True)
    score_gradient = (probs * (dprob - delta)).astype(jnp.bfloat16)
    return (probs, score_gradient, delta)


def key_side(queries, grad_out, heads, probs, score_gradient, nkeys):
    dkey = jnp.einsum(
        "hqk,qhd->khd",
        score_gradient,
        split_heads(queries, heads),
        preferred_element_type=jnp.float32,
    )
    dvalue = jnp.einsum(
        "hqk,qhd->khd",
        probs.astype(jnp.bfloat16),
        split_heads(grad_out, heads),
        preferred_element_type=jnp.float32,
    )
    return (dkey.reshape(nkeys, -1), dvalue.reshape(nkeys, -1))


def attend_back(queries, keys, values, heads, extra, keep, lse, grad_out):
    probs, score_gradient, delta = score_grads(
        queries, keys, values, heads, extra, keep, lse, grad_out, None
    )
    dquery = jnp.einsum(
        "hqk,khd->qhd", score_gradient, split_heads(keys, heads), preferred_element_type=jnp.float32
    )
    dkey, dvalue = key_side(queries, grad_out, heads, probs, score_gradient, keys.shape[0])
    return (dquery.reshape(queries.shape[0], -1), dkey, dvalue, score_gradient)


def per_device(
    tokens,
    encoder,
    cotangent,
    buckets,
    pairing,
    norm_one,
    self_query,
    self_key,
    self_value,
    self_output,
    bias_table,
    norm_two,
    cross_query,
    cross_key,
    cross_value,
    cross_output,
    norm_three,
    ff_gate,
    ff_up,
    ff_down,
):
    bf16 = jnp.bfloat16
    float_thirtytwo = jnp.float32
    whole = (
        lax.all_gather(norm_one, "fsdp", axis=0, tiled=True),
        lax.all_gather(self_query, "fsdp", axis=0, tiled=True),
        lax.all_gather(self_key, "fsdp", axis=0, tiled=True),
        lax.all_gather(self_value, "fsdp", axis=0, tiled=True),
        lax.all_gather(self_output, "fsdp", axis=0, tiled=True),
        lax.all_gather(bias_table, "fsdp", axis=0, tiled=True),
        lax.all_gather(norm_two, "fsdp", axis=0, tiled=True),
        lax.all_gather(cross_query, "fsdp", axis=0, tiled=True),
        lax.all_gather(cross_key, "fsdp", axis=0, tiled=True),
        lax.all_gather(cross_value, "fsdp", axis=0, tiled=True),
        lax.all_gather(cross_output, "fsdp", axis=0, tiled=True),
        lax.all_gather(norm_three, "fsdp", axis=0, tiled=True),
        lax.all_gather(ff_gate, "fsdp", axis=0, tiled=True),
        lax.all_gather(ff_up, "fsdp", axis=0, tiled=True),
        lax.all_gather(ff_down, "fsdp", axis=0, tiled=True),
    )
    (
        g_one,
        w_q,
        w_k,
        w_v,
        w_o,
        relative_bias_table,
        g_two,
        c_q,
        c_k,
        c_v,
        c_o,
        g_three,
        w_gate,
        w_up,
        w_down,
    ) = whole
    g_one = g_one.astype(float_thirtytwo)
    g_two = g_two.astype(float_thirtytwo)
    g_three = g_three.astype(float_thirtytwo)
    heads = relative_bias_table.shape[1]
    nbuckets = relative_bias_table.shape[0]
    rows_in = tokens[0].astype(float_thirtytwo)
    hidden_states = encoder[0]
    incoming = cotangent[0]
    count = rows_in.shape[0]
    block = count // 2
    groups = lax.axis_size("ctx")
    seq_len = count * groups
    mine = lax.axis_index("ctx")
    own_starts = jnp.stack([pairing[mine], 2 * groups - 1 - pairing[mine]])
    offs = jnp.arange(block, dtype=jnp.int32)
    query_pos = (own_starts[:, None] * block + offs[None, :]).reshape(-1)
    all_starts = jnp.stack([pairing, 2 * groups - 1 - pairing], axis=1).reshape(-1)
    key_pos = (all_starts[:, None] * block + offs[None, :]).reshape(-1)
    onehot, keep = pair_buckets(buckets, query_pos, key_pos, seq_len, nbuckets)
    position_bias = pair_bias(onehot, relative_bias_table)
    a_one, norm_one_back = jax.vjp(norm_apply, rows_in, g_one)
    a_one = a_one.astype(bf16)
    query = product(a_one, w_q).astype(bf16)
    key_own = product(a_one, w_k).astype(bf16)
    value_own = product(a_one, w_v).astype(bf16)
    key_all, value_all = (
        lax.all_gather(key_own, "ctx", axis=0, tiled=True),
        lax.all_gather(value_own, "ctx", axis=0, tiled=True),
    )
    attended, self_lse = attend(query, key_all, value_all, heads, position_bias, keep)
    attended = attended.astype(bf16)
    second = rows_in + product(attended, w_o)
    a_two, norm_two_back = jax.vjp(norm_apply, second, g_two)
    a_two = a_two.astype(bf16)
    cross_q = product(a_two, c_q).astype(bf16)
    key_part = product(hidden_states, c_k).astype(bf16)
    value_part = product(hidden_states, c_v).astype(bf16)
    cross_k, cross_v = (
        lax.all_gather(key_part, "ctx", axis=0, tiled=True),
        lax.all_gather(value_part, "ctx", axis=0, tiled=True),
    )
    cross_o, cross_lse = attend(cross_q, cross_k, cross_v, heads, None, None)
    cross_o = cross_o.astype(bf16)
    third = second + product(cross_o, c_o)
    a_three, norm_three_back = jax.vjp(norm_apply, third, g_three)
    a_three = a_three.astype(bf16)
    gate = product(a_three, w_gate)
    up_val = product(a_three, w_up)
    hidden, geglu_back = jax.vjp(
        lambda left, right: jax.nn.gelu(left, approximate=True) * right, gate, up_val
    )
    hidden = hidden.astype(bf16)
    result = third + product(hidden, w_down)
    grad_hidden = through(incoming, w_down)
    grad_down = weight_grad(hidden, incoming)
    grad_gate, grad_up = geglu_back(grad_hidden)
    grad_gate = grad_gate.astype(bf16)
    grad_up = grad_up.astype(bf16)
    grad_w_gate = weight_grad(a_three, grad_gate)
    grad_w_up = weight_grad(a_three, grad_up)
    grad_a_three = through(grad_gate, w_gate) + through(grad_up, w_up)
    part_three, grad_g_three = norm_three_back(grad_a_three)
    grad_third = incoming.astype(float_thirtytwo) + part_three
    branch_two = grad_third.astype(bf16)
    grad_c_o = weight_grad(cross_o, branch_two)
    grad_cross_o = through(branch_two, c_o).astype(bf16)
    dcq, dck_all, dcv_all, unused = attend_back(
        cross_q, cross_k, cross_v, heads, None, None, cross_lse, grad_cross_o
    )
    dck, dcv = (
        lax.psum_scatter(
            dck_all.astype(jnp.bfloat16), "ctx", scatter_dimension=0, tiled=True
        ).astype(jnp.float32),
        lax.psum_scatter(
            dcv_all.astype(jnp.bfloat16), "ctx", scatter_dimension=0, tiled=True
        ).astype(jnp.float32),
    )
    dcq = dcq.astype(bf16)
    dck = dck.astype(bf16)
    dcv = dcv.astype(bf16)
    grad_states = through(dck, c_k) + through(dcv, c_v)
    grad_c_q = weight_grad(a_two, dcq)
    grad_c_k = weight_grad(hidden_states, dck)
    grad_c_v = weight_grad(hidden_states, dcv)
    part_two, grad_g_two = norm_two_back(through(dcq, c_q))
    grad_second = grad_third + part_two
    branch_one = grad_second.astype(bf16)
    grad_w_o = weight_grad(attended, branch_one)
    grad_attended = through(branch_one, w_o).astype(bf16)
    dq, dk_all, dv_all, score_gradient = attend_back(
        query, key_all, value_all, heads, position_bias, keep, self_lse, grad_attended
    )
    dk, dv = (
        lax.psum_scatter(
            dk_all.astype(jnp.bfloat16), "ctx", scatter_dimension=0, tiled=True
        ).astype(jnp.float32),
        lax.psum_scatter(
            dv_all.astype(jnp.bfloat16), "ctx", scatter_dimension=0, tiled=True
        ).astype(jnp.float32),
    )
    dq = dq.astype(bf16)
    dk = dk.astype(bf16)
    dv = dv.astype(bf16)
    bucket_bias_gradient = table_gradient(score_gradient, onehot)
    grad_w_q = weight_grad(a_one, dq)
    grad_w_k = weight_grad(a_one, dk)
    grad_w_v = weight_grad(a_one, dv)
    grad_a_one = through(dq, w_q) + through(dk, w_k) + through(dv, w_v)
    part_one, grad_g_one = norm_one_back(grad_a_one)
    grad_rows = grad_second + part_one
    shards = (
        lax.psum_scatter(
            grad_g_one.astype(jnp.bfloat16), "fsdp", scatter_dimension=0, tiled=True
        ).astype(jnp.float32),
        lax.psum_scatter(
            grad_w_q.astype(jnp.bfloat16), "fsdp", scatter_dimension=0, tiled=True
        ).astype(jnp.float32),
        lax.psum_scatter(
            grad_w_k.astype(jnp.bfloat16), "fsdp", scatter_dimension=0, tiled=True
        ).astype(jnp.float32),
        lax.psum_scatter(
            grad_w_v.astype(jnp.bfloat16), "fsdp", scatter_dimension=0, tiled=True
        ).astype(jnp.float32),
        lax.psum_scatter(
            grad_w_o.astype(jnp.bfloat16), "fsdp", scatter_dimension=0, tiled=True
        ).astype(jnp.float32),
        lax.psum_scatter(
            bucket_bias_gradient.astype(jnp.bfloat16), "fsdp", scatter_dimension=0, tiled=True
        ).astype(jnp.float32),
        lax.psum_scatter(
            grad_g_two.astype(jnp.bfloat16), "fsdp", scatter_dimension=0, tiled=True
        ).astype(jnp.float32),
        lax.psum_scatter(
            grad_c_q.astype(jnp.bfloat16), "fsdp", scatter_dimension=0, tiled=True
        ).astype(jnp.float32),
        lax.psum_scatter(
            grad_c_k.astype(jnp.bfloat16), "fsdp", scatter_dimension=0, tiled=True
        ).astype(jnp.float32),
        lax.psum_scatter(
            grad_c_v.astype(jnp.bfloat16), "fsdp", scatter_dimension=0, tiled=True
        ).astype(jnp.float32),
        lax.psum_scatter(
            grad_c_o.astype(jnp.bfloat16), "fsdp", scatter_dimension=0, tiled=True
        ).astype(jnp.float32),
        lax.psum_scatter(
            grad_g_three.astype(jnp.bfloat16), "fsdp", scatter_dimension=0, tiled=True
        ).astype(jnp.float32),
        lax.psum_scatter(
            grad_w_gate.astype(jnp.bfloat16), "fsdp", scatter_dimension=0, tiled=True
        ).astype(jnp.float32),
        lax.psum_scatter(
            grad_w_up.astype(jnp.bfloat16), "fsdp", scatter_dimension=0, tiled=True
        ).astype(jnp.float32),
        lax.psum_scatter(
            grad_down.astype(jnp.bfloat16), "fsdp", scatter_dimension=0, tiled=True
        ).astype(jnp.float32),
    )
    totals = (
        lax.psum(shards[0].astype(jnp.bfloat16), "ctx").astype(jnp.float32),
        lax.psum(shards[1].astype(jnp.bfloat16), "ctx").astype(jnp.float32),
        lax.psum(shards[2].astype(jnp.bfloat16), "ctx").astype(jnp.float32),
        lax.psum(shards[3].astype(jnp.bfloat16), "ctx").astype(jnp.float32),
        lax.psum(shards[4].astype(jnp.bfloat16), "ctx").astype(jnp.float32),
        lax.psum(shards[5].astype(jnp.bfloat16), "ctx").astype(jnp.float32),
        lax.psum(shards[6].astype(jnp.bfloat16), "ctx").astype(jnp.float32),
        lax.psum(shards[7].astype(jnp.bfloat16), "ctx").astype(jnp.float32),
        lax.psum(shards[8].astype(jnp.bfloat16), "ctx").astype(jnp.float32),
        lax.psum(shards[9].astype(jnp.bfloat16), "ctx").astype(jnp.float32),
        lax.psum(shards[10].astype(jnp.bfloat16), "ctx").astype(jnp.float32),
        lax.psum(shards[11].astype(jnp.bfloat16), "ctx").astype(jnp.float32),
        lax.psum(shards[12].astype(jnp.bfloat16), "ctx").astype(jnp.float32),
        lax.psum(shards[13].astype(jnp.bfloat16), "ctx").astype(jnp.float32),
        lax.psum(shards[14].astype(jnp.bfloat16), "ctx").astype(jnp.float32),
    )
    return (
        result.astype(bf16)[None],
        grad_rows[None],
        grad_states[None],
        totals[0],
        totals[1],
        totals[2],
        totals[3],
        totals[4],
        totals[5],
        totals[6],
        totals[7],
        totals[8],
        totals[9],
        totals[10],
        totals[11],
        totals[12],
        totals[13],
        totals[14],
    )


def solution(mesh):
    placed = (
        P("fsdp", "ctx", None),
        P("fsdp", "ctx", None),
        P("fsdp", "ctx", None),
        P(),
        P(),
        P("fsdp"),
        P("fsdp", None),
        P("fsdp", None),
        P("fsdp", None),
        P("fsdp", None),
        P("fsdp", None),
        P("fsdp"),
        P("fsdp", None),
        P("fsdp", None),
        P("fsdp", None),
        P("fsdp", None),
        P("fsdp"),
        P("fsdp", None),
        P("fsdp", None),
        P("fsdp", None),
    )
    return jax.shard_map(
        per_device,
        mesh=mesh,
        in_specs=placed,
        out_specs=(
            P("fsdp", "ctx", None),
            P("fsdp", "ctx", None),
            P("fsdp", "ctx", None),
            P("fsdp"),
            P("fsdp", None),
            P("fsdp", None),
            P("fsdp", None),
            P("fsdp", None),
            P("fsdp", None),
            P("fsdp"),
            P("fsdp", None),
            P("fsdp", None),
            P("fsdp", None),
            P("fsdp", None),
            P("fsdp"),
            P("fsdp", None),
            P("fsdp", None),
            P("fsdp", None),
        ),
        check_vma=False,
    )
```

profile of v0, /device:TPU:1, one launch (start us, length us, event | category | flops | bytes accessed | tf_op | source)
XLA Modules:
  0.0 1417.2 jit_solution(13993626436235360968)
XLA Ops:
  15.2 11.8 all-reduce.10
  28.6 13.3 all-gather.20.cloned.1.call-done
  44.4 28.8 %all-gather.14.cloned.1.call-done = bf16[768,768]{1,0:T(8,128)(2,1)} async-done(((bf16[192,768]{1,0:T(8,128)(2,1)}), bf16[768,768]{1,0:T(8,128)(2,1)}) %all-gather.14.cloned.1.call-update) | async-done | bytes 1179664 | tf_op jit(solution)/shard_map/all_gather | solution.py:140
  83.4 520.8 %gather_fusion = s32[131072]{0:T(1024)S(1)} fusion(s32[1024]{0:T(1024)S(1)} %copy-done.1, s32[131072]{0:T(1024)S(1)} %broadcast_clamp_fusion), kind=kCustom, calls=%fused_computation | custom fusion | bytes 1572864 | tf_op jit(solution)/shard_map/jit(_take)/gather | solution.py:31
  605.9 9.3 all_gather.63
  615.2 5.5 fusion.3
  620.7 8.4 copy.84
  632.6 14.1 all_gather.70
  649.4 10.6 all_gather.66
  663.0 4.7 fusion.94
  673.5 4.8 fusion.32
  698.5 5.0 multiply_convert_fusion.2
  734.1 4.8 multiply_reduce_fusion
  752.7 33.1 %reduce-scatter.50.cloned.1.call-done = bf16[64,768]{1,0:T(8,128)(2,1)} async-done(((bf16[512,768]{1,0:T(8,128)(2,1)}), bf16[64,768]{1,0:T(8,128)(2,1)}) %reduce-scatter.50.cloned.1.call-update) | async-done | bytes 98320
  803.8 24.0 %reduce-scatter.48.cloned.1.call-done = bf16[128,768]{1,0:T(8,128)(2,1)} async-done(((bf16[1024,768]{1,0:T(8,128)(2,1)}), bf16[128,768]{1,0:T(8,128)(2,1)}) %reduce-scatter.48.cloned.1.call-update) | async-done | bytes 196624
  830.4 39.5 %reduce-scatter.46.cloned.1.call-done = bf16[128,768]{1,0:T(8,128)(2,1)} async-done(((bf16[1024,768]{1,0:T(8,128)(2,1)}), bf16[128,768]{1,0:T(8,128)(2,1)}) %reduce-scatter.46.cloned.1.call-update) | async-done | bytes 196624
  885.6 8.0 copy.90
  896.9 4.3 reduce-scatter.56.cloned.1.call-done
  903.0 28.4 %reduce-scatter.54.cloned.1.call-done = bf16[192,768]{1,0:T(8,128)(2,1)} async-done(((bf16[768,768]{1,0:T(8,128)(2,1)}), bf16[192,768]{1,0:T(8,128)(2,1)}) %reduce-scatter.54.cloned.1.call-update) | async-done | bytes 294928
  933.3 28.2 %reduce-scatter.36.cloned.1.call-done = bf16[192,768]{1,0:T(8,128)(2,1)} async-done(((bf16[768,768]{1,0:T(8,128)(2,1)}), bf16[192,768]{1,0:T(8,128)(2,1)}) %reduce-scatter.36.cloned.1.call-update) | async-done | bytes 294928 | tf_op jit(solution)/shard_map/reduce_scatter | solution.py:302
  961.5 30.2 %reduce-scatter.38.cloned.1.call-done = bf16[192,768]{1,0:T(8,128)(2,1)} async-done(((bf16[768,768]{1,0:T(8,128)(2,1)}), bf16[192,768]{1,0:T(8,128)(2,1)}) %reduce-scatter.38.cloned.1.call-update) | async-done | bytes 294928 | tf_op jit(solution)/shard_map/reduce_scatter | solution.py:311
  991.7 30.2 %reduce-scatter.34.cloned.1.call-done = bf16[192,768]{1,0:T(8,128)(2,1)} async-done(((bf16[768,768]{1,0:T(8,128)(2,1)}), bf16[192,768]{1,0:T(8,128)(2,1)}) %reduce-scatter.34.cloned.1.call-update) | async-done | bytes 294928 | tf_op jit(solution)/shard_map/reduce_scatter | solution.py:293
  1022.0 30.8 %reduce-scatter.28.cloned.1.call-done = bf16[192,768]{1,0:T(8,128)(2,1)} async-done(((bf16[768,768]{1,0:T(8,128)(2,1)}), bf16[192,768]{1,0:T(8,128)(2,1)}) %reduce-scatter.28.cloned.1.call-update) | async-done | bytes 294928 | tf_op jit(solution)/shard_map/reduce_scatter | solution.py:284
  1052.8 30.1 %reduce-scatter.32.cloned.1.call-done = bf16[192,768]{1,0:T(8,128)(2,1)} async-done(((bf16[768,768]{1,0:T(8,128)(2,1)}), bf16[192,768]{1,0:T(8,128)(2,1)}) %reduce-scatter.32.cloned.1.call-update) | async-done | bytes 294928 | tf_op jit(solution)/shard_map/reduce_scatter | solution.py:290
  1082.9 30.8 %reduce-scatter.30.cloned.1.call-done = bf16[192,768]{1,0:T(8,128)(2,1)} async-done(((bf16[768,768]{1,0:T(8,128)(2,1)}), bf16[192,768]{1,0:T(8,128)(2,1)}) %reduce-scatter.30.cloned.1.call-update) | async-done | bytes 294928 | tf_op jit(solution)/shard_map/reduce_scatter | solution.py:287
  1113.7 61.2 %reduce-scatter.40.cloned.1.call-done = bf16[192,2048]{1,0:T(8,128)(2,1)} async-done(((bf16[768,2048]{1,0:T(8,128)(2,1)}), bf16[192,2048]{1,0:T(8,128)(2,1)}) %reduce-scatter.40.cloned.1.call-update) | async-done | bytes 786448 | tf_op jit(solution)/shard_map/reduce_scatter | solution.py:317
  1174.8 62.5 %reduce-scatter.42.cloned.1.call-done = bf16[192,2048]{1,0:T(8,128)(2,1)} async-done(((bf16[768,2048]{1,0:T(8,128)(2,1)}), bf16[192,2048]{1,0:T(8,128)(2,1)}) %reduce-scatter.42.cloned.1.call-update) | async-done | bytes 786448 | tf_op jit(solution)/shard_map/reduce_scatter | solution.py:320
  1237.3 62.6 %reduce-scatter.44.cloned.1.call-done = bf16[512,768]{1,0:T(8,128)(2,1)} async-done(((bf16[2048,768]{1,0:T(8,128)(2,1)}), bf16[512,768]{1,0:T(8,128)(2,1)}) %reduce-scatter.44.cloned.1.call-update) | async-done | bytes 786448 | tf_op jit(solution)/shard_map/reduce_scatter | solution.py:323
  1301.0 5.4 fusion.38
  1309.4 14.1 all-reduce.9
  1323.7 15.7 %all-reduce.7 = (bf16[192]{0:T(256)(128)(2,1)S(1)}, bf16[8,12]{1,0:T(8,128)(2,1)S(1)}, bf16[192]{0:T(256)(128)(2,1)S(1)}, bf16[192]{0:T(256)(128)(2,1)S(1)}) all-reduce(bf16[192]{0:T(256)(128)(2,1)S(1)} %dynamic-slice.4, bf16[8,12]{1,0:T(8,128)(2,1)S(1)} %constant_dynamic-slice_fusion, ...), channel_id=1, replica_groups=mesh['ctx'=8,'fsdp'=4] {'ctx'}, use_global_device_ids=true, to_apply=%region_18.19 | all-reduce | flops 672 | bytes 2688 | tf_op jit(solution)/shard_map/psum | solution.py:328
  1342.7 54.3 %all-reduce.13.cloned.1.call-done = (bf16[192,768]{0,1:T(8,128)(2,1)}, bf16[192,768]{0,1:T(8,128)(2,1)}, bf16[192,768]{1,0:T(8,128)(2,1)}, bf16[192,768]{1,0:T(8...) async-done(((bf16[192,768]{0,1:T(8,128)(2,1)}, ...) | async-done | bytes 4718608 | tf_op jit(solution)/shard_map/psum | solution.py:336
  (329 shorter events, 164.1 us)
Async XLA Ops:
  7.2 623.8 %copy-start = (bf16[1,64,768]{2,1,0:T(8,128)(2,1)S(1)}, bf16[1,64,768]{2,1,0:T(8,128)(2,1)}, u32[]{:S(2)}) copy-start(bf16[1,64,768]{2,1,0:T(8,128)(2,1)} %param.21) | copy-start | bytes 294916
  7.2 34.7 %all-gather.20.cloned.1.call-start = ((), (), s32[]{:S(2)}) async-start(), calls=%async_computation.18 | async-start | bytes 1474560 | tf_op jit(solution)/shard_map/all_gather | solution.py:139
  8.0 65.2 %all-gather.14.cloned.1.call-start = ((), (), s32[]{:S(2)}) async-start(), calls=%async_computation.15 | async-start | bytes 1474560 | tf_op jit(solution)/shard_map/all_gather | solution.py:140
  8.7 620.4 %all-gather.18.cloned.1.call-start = ((), (), s32[]{:S(2)}) async-start(), calls=%async_computation.17 | async-start | bytes 1474560 | tf_op jit(solution)/shard_map/all_gather | solution.py:138
  9.4 621.5 %all-gather.30.cloned.1.call-start = ((), (), s32[]{:S(2)}) async-start(), calls=%async_computation.23 | async-start | bytes 1474560 | tf_op jit(solution)/shard_map/all_gather | solution.py:145
  10.0 637.8 %all-gather.26.cloned.1.call-start = ((), (), s32[]{:S(2)}) async-start(), calls=%async_computation.21 | async-start | bytes 1474560 | tf_op jit(solution)/shard_map/all_gather | solution.py:146
  10.6 650.7 %all-gather.22.cloned.1.call-start = ((), (), s32[]{:S(2)}) async-start(), calls=%async_computation.19 | async-start | bytes 1769472 | tf_op jit(solution)/shard_map/all_gather | solution.py:196
  44.3 627.4 %all-gather.16.cloned.1.call-start = ((), (), s32[]{:S(2)}) async-start(), calls=%async_computation.16 | async-start | bytes 1769472 | tf_op jit(solution)/shard_map/all_gather | solution.py:197
  75.5 602.8 %all-gather.24.cloned.1.call-start = ((), (), s32[]{:S(2)}) async-start(), calls=%async_computation.20 | async-start | bytes 1474560 | tf_op jit(solution)/shard_map/all_gather | solution.py:141
  76.3 603.9 %all-gather.28.cloned.1.call-start = ((), (), s32[]{:S(2)}) async-start(), calls=%async_computation.22 | async-start | bytes 1474560 | tf_op jit(solution)/shard_map/all_gather | solution.py:144
  77.0 610.8 %all-gather.32.cloned.1.call-start = ((), (), s32[]{:S(2)}) async-start(), calls=%async_computation.24 | async-start | bytes 1474560 | tf_op jit(solution)/shard_map/all_gather | solution.py:147
  77.6 613.6 %all-gather.34.cloned.1.call-start = ((), (), s32[]{:S(2)}) async-start(), calls=%async_computation.25 | async-start | bytes 3932160 | tf_op jit(solution)/shard_map/all_gather | solution.py:149
  78.3 616.5 %all-gather.36.cloned.1.call-start = ((), (), s32[]{:S(2)}) async-start(), calls=%async_computation.26 | async-start | bytes 3932160 | tf_op jit(solution)/shard_map/all_gather | solution.py:150
  78.9 619.5 %all-gather.38.cloned.1.call-start = ((), (), s32[]{:S(2)}) async-start(), calls=%async_computation.27 | async-start | bytes 3932160 | tf_op jit(solution)/shard_map/all_gather | solution.py:151
  79.7 668.1 %reduce-scatter.52.cloned.1.call-start = ((), (), s32[]{:S(2)}) async-start(), calls=%async_computation.40 | async-start | bytes 884736
  81.9 522.4 %copy-start.62 = (s32[128]{0:T(128)}, s32[128]{0:T(128)S(1)}, u32[]{:S(2)}) copy-start(s32[128]{0:T(128)S(1)} %add.228) | copy-start | bytes 1540
  82.2 522.1 %copy-start.59 = (s32[1024]{0:T(1024)}, s32[1024]{0:T(1024)S(1)}, u32[]{:S(2)}) copy-start(s32[1024]{0:T(1024)S(1)} %add.232) | copy-start | bytes 12292
  715.9 69.9 %reduce-scatter.50.cloned.1.call-start = ((), (), s32[]{:S(2)}) async-start(), calls=%async_computation.39 | async-start | bytes 884736
  724.0 103.8 %reduce-scatter.48.cloned.1.call-start = ((), (), s32[]{:S(2)}) async-start(), calls=%async_computation.38 | async-start | bytes 1769472
  734.1 135.9 %reduce-scatter.46.cloned.1.call-start = ((), (), s32[]{:S(2)}) async-start(), calls=%async_computation.37 | async-start | bytes 1769472
  747.0 154.1 %reduce-scatter.56.cloned.1.call-start = ((), (), s32[]{:S(2)}) async-start(), calls=%async_computation.42 | async-start | bytes 1474560
  752.6 178.8 %reduce-scatter.54.cloned.1.call-start = ((), (), s32[]{:S(2)}) async-start(), calls=%async_computation.41 | async-start | bytes 1474560
  790.6 170.9 %reduce-scatter.36.cloned.1.call-start = ((), (), s32[]{:S(2)}) async-start(), calls=%async_computation.32 | async-start | bytes 1474560 | tf_op jit(solution)/shard_map/reduce_scatter | solution.py:302
  793.3 198.4 %reduce-scatter.38.cloned.1.call-start = ((), (), s32[]{:S(2)}) async-start(), calls=%async_computation.33 | async-start | bytes 1474560 | tf_op jit(solution)/shard_map/reduce_scatter | solution.py:311
  796.0 226.0 %reduce-scatter.34.cloned.1.call-start = ((), (), s32[]{:S(2)}) async-start(), calls=%async_computation.31 | async-start | bytes 1474560 | tf_op jit(solution)/shard_map/reduce_scatter | solution.py:293
  798.7 254.1 %reduce-scatter.28.cloned.1.call-start = ((), (), s32[]{:S(2)}) async-start(), calls=%async_computation.28 | async-start | bytes 1474560 | tf_op jit(solution)/shard_map/reduce_scatter | solution.py:284
  803.7 279.2 %reduce-scatter.32.cloned.1.call-start = ((), (), s32[]{:S(2)}) async-start(), calls=%async_computation.30 | async-start | bytes 1474560 | tf_op jit(solution)/shard_map/reduce_scatter | solution.py:290
  830.4 283.3 %reduce-scatter.30.cloned.1.call-start = ((), (), s32[]{:S(2)}) async-start(), calls=%async_computation.29 | async-start | bytes 1474560 | tf_op jit(solution)/shard_map/reduce_scatter | solution.py:287
  872.5 302.4 %reduce-scatter.40.cloned.1.call-start = ((), (), s32[]{:S(2)}) async-start(), calls=%async_computation.34 | async-start | bytes 3932160 | tf_op jit(solution)/shard_map/reduce_scatter | solution.py:317
  876.3 361.0 %reduce-scatter.42.cloned.1.call-start = ((), (), s32[]{:S(2)}) async-start(), calls=%async_computation.35 | async-start | bytes 3932160 | tf_op jit(solution)/shard_map/reduce_scatter | solution.py:320
  880.3 419.6 %reduce-scatter.44.cloned.1.call-start = ((), (), s32[]{:S(2)}) async-start(), calls=%async_computation.36 | async-start | bytes 3932160 | tf_op jit(solution)/shard_map/reduce_scatter | solution.py:323
  884.2 512.8 %all-reduce.13.cloned.1.call-start = ((), (), s32[]{:S(2)}) async-start(), calls=%async_computation.43 | async-start | bytes 9830400 | tf_op jit(solution)/shard_map/psum | solution.py:336
  (66 other events, 1364.3 us)
Sparse Core Ops, SparseCore 0:
  9.6 32.2 all-gather.19
  43.5 29.6 all-gather.13
  74.8 29.5 all-gather.17
  105.8 29.6 all-gather.29
  136.9 29.5 all-gather.25
  168.8 25.8 all-gather.21
  197.1 25.6 all-gather.15
  224.4 29.4 all-gather.23
  255.5 29.5 all-gather.27
  286.5 29.5 all-gather.31
  317.7 63.1 all-gather.33
  382.3 62.1 all-gather.35
  446.1 62.1 all-gather.37
  716.0 31.7 reduce-scatter.51
  750.8 34.9 reduce-scatter.49
  788.9 38.7 reduce-scatter.47
  831.5 38.4 reduce-scatter.45
  872.1 28.9 reduce-scatter.55
  903.5 27.8 reduce-scatter.53
  933.5 27.8 reduce-scatter.35
  963.8 27.8 reduce-scatter.37
  994.0 27.8 reduce-scatter.33
  1024.9 27.8 reduce-scatter.27
  1054.9 27.8 reduce-scatter.31
  1085.8 27.8 reduce-scatter.29
  1115.8 58.9 reduce-scatter.39
  1177.0 60.2 reduce-scatter.41
  1239.6 60.2 reduce-scatter.43
  1305.3 91.7 all-reduce.12
where the time goes:
time: 1430 us; the launch traced here: 1420 us
  waiting for transfers between devices  600 us (42%)
  local copies, waits for them, and re-layouts  579 us (40%)
  matrix products  116 us (8%)
  blocking collectives  75.6 us (5%)
  other arithmetic  26.6 us (2%)
  between operations  18 us (1%)
    gather x2, local copies, waits for them, and re-layouts, pair_buckets(): bucket_ids = jnp.take(buckets, spots)  521 us
    unnamed x35, waiting for transfers between devices  137 us
    reduce_scatter x1, waiting for transfers between devices, per_device(): lax.psum_scatter(grad_down.astype(jnp.bfloat16), 'fsdp', scatter_dimensio...  62.6 us
    reduce_scatter x1, waiting for transfers between devices, per_device(): lax.psum_scatter(grad_w_up.astype(jnp.bfloat16), 'fsdp', scatter_dimensio...  62.5 us
    reduce_scatter x1, waiting for transfers between devices, per_device(): lax.psum_scatter(grad_w_gate.astype(jnp.bfloat16), 'fsdp', scatter_dimens...  61.2 us
    psum x1, waiting for transfers between devices, per_device(): lax.psum(shards[8].astype(jnp.bfloat16), 'ctx').astype(jnp.float32)  54.3 us
    unnamed x160, local copies, waits for them, and re-layouts  32 us
    dot_general x11, matrix products, weight_grad(): return jnp.einsum('td,tf->df', a, grad, preferred_element_type=jnp.float32)  30.9 us
  transfers between devices with their start and end apart: 29, of which 18 were waited for; matrix products, arithmetic and copies ran while one was open for 48% of the time, Pallas kernels for 0%

commit v1 on v0

v1 whole, which is shorter than its diff:
```python
import functools
import math

import jax
import jax.numpy as jnp
from jax import lax
from jax.experimental import pallas as pl
from jax.experimental.pallas import tpu as pltpu
from jax.sharding import PartitionSpec as P

BF = jnp.bfloat16
F32 = jnp.float32
LANES = 128
VMEM_LIMIT = 48 * 1024 * 1024
LAST = (((1,), (1,)), ((), ()))
FIRST = (((0,), (0,)), ((), ()))
PLAIN = (((1,), (0,)), ((), ()))


def norm_apply(v, g):
    return v * lax.rsqrt(jnp.mean(v * v, axis=-1, keepdims=True) + 1e-06) * g


def product(a, w):
    return jnp.dot(a, w, preferred_element_type=F32)


def through(grad, w):
    return lax.dot_general(grad, w, LAST, preferred_element_type=F32)


def weight_grad(a, grad):
    return lax.dot_general(a, grad, FIRST, preferred_element_type=F32)


def dot(a, b, dims):
    return lax.dot_general(a, b, dims, preferred_element_type=F32)


def two_heads(block):
    half = block.shape[1] // 2
    low = lax.broadcasted_iota(jnp.int32, block.shape, 1) < half
    zero = jnp.zeros_like(block)
    return jnp.concatenate([jnp.where(low, block, zero), jnp.where(low, zero, block)], axis=0)


def join_heads(rows):
    n = rows.shape[0] // 2
    low = lax.broadcasted_iota(jnp.int32, (n, rows.shape[1]), 1) < rows.shape[1] // 2
    return jnp.where(low, rows[:n], rows[n:])


def to_positions(blocks_ref, source, target, block):
    for i in range(source.shape[0] // block):
        spot = pl.multiple_of(blocks_ref[i] * block, block)
        target[pl.ds(spot, block), :] = source[i * block : (i + 1) * block, :]


def from_positions(blocks_ref, source, target, block):
    for i in range(target.shape[0] // block):
        spot = pl.multiple_of(blocks_ref[i] * block, block)
        target[i * block : (i + 1) * block, :] = source[pl.ds(spot, block), :].astype(target.dtype)


def sheared(line, block):
    sublane = lax.broadcasted_iota(jnp.int32, line.shape, 0)
    for bit in (1, 2, 4):
        line = jnp.where(sublane & bit != 0, pltpu.roll(line, bit, 1), line)
    return jnp.concatenate([line if i == 0 else pltpu.roll(line, i, 1) for i in range(0, block, 8)], axis=0)


def self_forward_kernel(blocks_ref, own_ref, q_ref, k_ref, v_ref, bias_ref, o_ref, p_ref, ks, vs):
    rows = q_ref.shape[0]
    block = rows // 2
    nkeys = k_ref.shape[0]
    to_positions(blocks_ref, k_ref, ks, block)
    to_positions(blocks_ref, v_ref, vs, block)
    scores = dot(two_heads(q_ref[...]), ks[...], LAST)
    column = lax.broadcasted_iota(jnp.int32, (block, nkeys), 1)
    row = lax.broadcasted_iota(jnp.int32, (block, nkeys), 0)
    for head in range(2):
        line = jnp.broadcast_to(bias_ref[0, head : head + 1, :], (8, nkeys))
        for part in range(2):
            start = own_ref[part] * block
            shear = sheared(pltpu.roll(line, start + 1, 1), block)
            at = head * rows + part * block
            s = jnp.where(column <= row + start, scores[at : at + block] + shear, -1e30)
            top = jnp.max(s, axis=-1, keepdims=True)
            expo = jnp.exp(s - top)
            total = jnp.sum(expo, axis=-1, keepdims=True)
            p_ref[0, at : at + block, :] = (expo / total).astype(BF)
    o_ref[...] = join_heads(dot(p_ref[0], vs[...], PLAIN)).astype(BF)


def cross_forward_kernel(q_ref, k_ref, v_ref, o_ref, p_ref):
    s = dot(two_heads(q_ref[...]), k_ref[...], LAST)
    top = jnp.max(s, axis=-1, keepdims=True)
    expo = jnp.exp(s - top)
    total = jnp.sum(expo, axis=-1, keepdims=True)
    p_ref[0] = (expo / total).astype(BF)
    o_ref[...] = join_heads(dot(p_ref[0], v_ref[...], PLAIN)).astype(BF)


def score_gradient(probs, dom, values):
    dp = dot(dom, values, LAST)
    p = probs.astype(F32)
    delta = jnp.sum(p * dp, axis=-1, keepdims=True)
    return (p * (dp - delta)).astype(BF)


def cross_backward_kernel(q_ref, k_ref, v_ref, do_ref, p_ref, dq_ref, dk_ref, dv_ref):
    dom = two_heads(do_ref[...])
    probs = p_ref[0]
    ds = score_gradient(probs, dom, v_ref[...])
    dq_ref[...] = join_heads(dot(ds, k_ref[...], PLAIN)).astype(BF)
    dk_ref[...] = dot(ds, two_heads(q_ref[...]), FIRST).astype(BF)
    dv_ref[...] = dot(probs, dom, FIRST).astype(BF)


def self_backward_kernel(
    blocks_ref, own_ref, q_ref, k_ref, v_ref, do_ref, p_ref, dq_ref, dk_ref, dv_ref, db_ref, ks, vs, acc
):
    rows = q_ref.shape[0]
    block = rows // 2
    nkeys = k_ref.shape[0]
    to_positions(blocks_ref, k_ref, ks, block)
    to_positions(blocks_ref, v_ref, vs, block)
    dom = two_heads(do_ref[...])
    probs = p_ref[0]
    ds = score_gradient(probs, dom, vs[...])
    dq_ref[...] = join_heads(dot(ds, ks[...], PLAIN)).astype(BF)
    acc[...] = dot(ds, two_heads(q_ref[...]), FIRST)
    from_positions(blocks_ref, acc, dk_ref, block)
    acc[...] = dot(probs, dom, FIRST)
    from_positions(blocks_ref, acc, dv_ref, block)
    for head in range(2):
        lines = None
        for part in range(2):
            at = head * rows + part * block
            x = ds[at : at + block].astype(F32)
            size = block
            while size > 1:
                size //= 2
                x = x[:size] + pltpu.roll(x[size:], nkeys - size, 1)
            x = pltpu.roll(jnp.broadcast_to(x, (8, nkeys)), nkeys - own_ref[part] * block - 1, 1)
            lines = x if lines is None else lines + x
        db_ref[0, head : head + 1, :] = lines[0:1]


def column_block(rows, offset):
    return pl.BlockSpec((rows, LANES), lambda i, *_: (0, offset + i))


def whole_block(a, b):
    return pl.BlockSpec((1, a, b), lambda i, *_: (i, 0, 0))


def params():
    return pltpu.CompilerParams(vmem_limit_bytes=VMEM_LIMIT)


def cost(rows, nkeys, width, products):
    return pl.CostEstimate(
        flops=4 * rows * nkeys * width * products,
        bytes_accessed=4 * rows * nkeys * (width // LANES) + 8 * nkeys * width,
        transcendentals=2 * rows * nkeys * (width // LANES),
    )


def self_forward(blocks, own, q, kv, bias):
    rows, width = q.shape
    nkeys = kv.shape[0]
    pairs = width // LANES
    return pl.pallas_call(
        self_forward_kernel,
        grid_spec=pltpu.PrefetchScalarGridSpec(
            num_scalar_prefetch=2,
            grid=(pairs,),
            in_specs=[
                column_block(rows, 0),
                column_block(nkeys, 0),
                column_block(nkeys, pairs),
                whole_block(2, nkeys),
            ],
            out_specs=[column_block(rows, 0), whole_block(2 * rows, nkeys)],
            scratch_shapes=[pltpu.VMEM((nkeys, LANES), BF), pltpu.VMEM((nkeys, LANES), BF)],
        ),
        out_shape=[
            jax.ShapeDtypeStruct((rows, width), BF),
            jax.ShapeDtypeStruct((pairs, 2 * rows, nkeys), BF),
        ],
        compiler_params=params(),
        cost_estimate=cost(rows, nkeys, width, 2),
        name="self_forward",
    )(blocks, own, q, kv, kv, bias)


def self_backward(blocks, own, q, kv, do, probs):
    rows, width = q.shape
    nkeys = kv.shape[0]
    pairs = width // LANES
    return pl.pallas_call(
        self_backward_kernel,
        grid_spec=pltpu.PrefetchScalarGridSpec(
            num_scalar_prefetch=2,
            grid=(pairs,),
            in_specs=[
                column_block(rows, 0),
                column_block(nkeys, 0),
                column_block(nkeys, pairs),
                column_block(rows, 0),
                whole_block(2 * rows, nkeys),
            ],
            out_specs=[
                column_block(rows, 0),
                column_block(nkeys, 0),
                column_block(nkeys, 0),
                whole_block(2, nkeys),
            ],
            scratch_shapes=[
                pltpu.VMEM((nkeys, LANES), BF),
                pltpu.VMEM((nkeys, LANES), BF),
                pltpu.VMEM((nkeys, LANES), F32),
            ],
        ),
        out_shape=[
            jax.ShapeDtypeStruct((rows, width), BF),
            jax.ShapeDtypeStruct((nkeys, width), BF),
            jax.ShapeDtypeStruct((nkeys, width), BF),
            jax.ShapeDtypeStruct((pairs, 2, nkeys), F32),
        ],
        compiler_params=params(),
        cost_estimate=cost(rows, nkeys, width, 5),
        name="self_backward",
    )(blocks, own, q, kv, kv, do, probs)


def cross_forward(q, kv):
    rows, width = q.shape
    nkeys = kv.shape[0]
    pairs = width // LANES
    return pl.pallas_call(
        cross_forward_kernel,
        grid=(pairs,),
        in_specs=[column_block(rows, 0), column_block(nkeys, 0), column_block(nkeys, pairs)],
        out_specs=[column_block(rows, 0), whole_block(2 * rows, nkeys)],
        out_shape=[
            jax.ShapeDtypeStruct((rows, width), BF),
            jax.ShapeDtypeStruct((pairs, 2 * rows, nkeys), BF),
        ],
        compiler_params=params(),
        cost_estimate=cost(rows, nkeys, width, 2),
        name="cross_forward",
    )(q, kv, kv)


def cross_backward(q, kv, do, probs):
    rows, width = q.shape
    nkeys = kv.shape[0]
    pairs = width // LANES
    return pl.pallas_call(
        cross_backward_kernel,
        grid=(pairs,),
        in_specs=[
            column_block(rows, 0),
            column_block(nkeys, 0),
            column_block(nkeys, pairs),
            column_block(rows, 0),
            whole_block(2 * rows, nkeys),
        ],
        out_specs=[column_block(rows, 0), column_block(nkeys, 0), column_block(nkeys, 0)],
        out_shape=[
            jax.ShapeDtypeStruct((rows, width), BF),
            jax.ShapeDtypeStruct((nkeys, width), BF),
            jax.ShapeDtypeStruct((nkeys, width), BF),
        ],
        compiler_params=params(),
        cost_estimate=cost(rows, nkeys, width, 5),
        name="cross_backward",
    )(q, kv, kv, do, probs)


class Net:
    def __init__(self):
        self.c = lax.axis_index("ctx")
        self.z = lax.axis_index("fsdp")
        self.nc = lax.axis_size("ctx")
        self.nz = lax.axis_size("fsdp")
        self.chips = self.nc // 2
        self.core = self.c % 2
        self.chip = self.c // 2

    def to_core(self, x):
        return lax.ppermute(x, "ctx", [(i, i ^ 1) for i in range(self.nc)])

    def to_chip(self, x, k):
        return lax.ppermute(x, "ctx", [(i, i ^ (2 * k)) for i in range(self.nc)])

    def along(self, x, s):
        n = self.nz
        return lax.ppermute(x, "fsdp", [(i, (i + s) % n) for i in range(n)])

    def gather_ctx(self, x):
        got = [x] + [self.to_chip(x, k) for k in range(1, self.chips)]
        mine = jnp.stack(got)
        other = self.to_core(mine)
        out = jnp.zeros((self.nc,) + x.shape, x.dtype)
        for k in range(self.chips):
            spot = 2 * (self.chip ^ k)
            out = lax.dynamic_update_index_in_dim(out, mine[k], spot + self.core, 0)
            out = lax.dynamic_update_index_in_dim(out, other[k], spot + 1 - self.core, 0)
        return out

    def gather_weights(self, piece):
        rows, cols = piece.shape
        parts = jnp.zeros((self.nz, rows, cols), piece.dtype)
        parts = lax.dynamic_update_index_in_dim(parts, piece, self.z, 0)
        for s in range(1, self.nz):
            got = self.along(piece, s)
            parts = lax.dynamic_update_index_in_dim(parts, got, (self.z + self.nz - s) % self.nz, 0)
        whole = self.gather_ctx(parts)
        return jnp.swapaxes(whole, 0, 1).reshape(self.nz * self.nc * rows, cols)

    def scatter_ctx(self, x):
        x = x.reshape((self.chips, 2) + x.shape[1:])
        keep = lax.dynamic_index_in_dim(x, self.core, 1, keepdims=False)
        give = lax.dynamic_index_in_dim(x, 1 - self.core, 1, keepdims=False)
        both = (keep.astype(F32) + self.to_core(give).astype(F32)).astype(BF)
        total = lax.dynamic_index_in_dim(both, self.chip, 0, keepdims=False).astype(F32)
        for k in range(1, self.chips):
            send = lax.dynamic_index_in_dim(both, self.chip ^ k, 0, keepdims=False)
            total = total + self.to_chip(send, k).astype(F32)
        return total

    def reduce_weights(self, grad):
        rows, cols = grad.shape
        each = rows // (self.nz * self.nc)
        x = grad.reshape(self.nz, self.nc, each, cols).swapaxes(0, 1)
        mine = self.scatter_ctx(x).astype(BF)
        total = lax.dynamic_index_in_dim(mine, self.z, 0, keepdims=False).astype(F32)
        for s in range(1, self.nz):
            send = lax.dynamic_index_in_dim(mine, (self.z + s) % self.nz, 0, keepdims=False)
            total = total + self.along(send, s).astype(F32)
        return self.gather_ctx(total.astype(BF)).reshape(self.nc * each, cols)


def per_device(
    tokens,
    encoder,
    cotangent,
    buckets,
    pairing,
    norm_one,
    self_query,
    self_key,
    self_value,
    self_output,
    bias_table,
    norm_two,
    cross_query,
    cross_key,
    cross_value,
    cross_output,
    norm_three,
    ff_gate,
    ff_up,
    ff_down,
):
    net = Net()
    nc, nz = net.nc, net.nz
    mine = net.c
    shard = self_query.shape[0]
    width = self_query.shape[1]
    hidden_width = ff_gate.shape[1]
    heads = bias_table.shape[1]
    pairs = width // LANES
    each = shard // nc
    down_each = ff_down.shape[0] // nc

    def rows_of(w):
        n = w.shape[0] // nc
        return lax.dynamic_slice_in_dim(w, mine * n, n, 0)

    table_size = bias_table.size
    extra_width = LANES * math.ceil((4 + table_size) / LANES)
    small = jnp.stack([norm_one, norm_two, norm_three], axis=1)
    small = jnp.pad(rows_of(small), ((0, 0), (0, extra_width - 3)))
    flat = jnp.pad(bias_table.reshape(1, -1), ((0, each - 1), (4, extra_width - 4 - table_size)))
    small = small + flat
    one = net.gather_weights(
        jnp.concatenate([rows_of(self_query), rows_of(self_key), rows_of(self_value), small], axis=1)
    )
    rows_all = net.gather_ctx(jnp.concatenate([tokens[0], encoder[0]], axis=0))
    two = net.gather_weights(
        jnp.concatenate(
            [rows_of(w) for w in (self_output, cross_query, cross_key, cross_value, cross_output)], axis=1
        )
    )
    w_gate = lax.all_gather(rows_of(ff_gate), ("fsdp", "ctx"), axis=0, tiled=True)
    w_up = lax.all_gather(rows_of(ff_up), ("fsdp", "ctx"), axis=0, tiled=True)
    w_down = lax.all_gather(rows_of(ff_down), ("fsdp", "ctx"), axis=0, tiled=True)

    w_q = one[:, :width]
    w_kv = one[:, width : 3 * width]
    extra = one[:, 3 * width :]
    gains = extra[:, :4].astype(F32).T
    g_one, g_two, g_three = gains[0], gains[1], gains[2]
    table = extra.reshape(nz, shard, extra_width)[:, 0, 4 : 4 + table_size].reshape(-1, heads)
    nbuckets = table.shape[0]
    w_o, c_q, c_kv, c_o = (
        two[:, :width],
        two[:, width : 2 * width],
        two[:, 2 * width : 4 * width],
        two[:, 4 * width :],
    )

    count = tokens.shape[1]
    block = count // 2
    seq_len = count * nc
    tokens_all = rows_all[:, :count].reshape(seq_len, width)
    states_all = rows_all[:, count:].reshape(-1, width)
    first = pairing[mine]
    own = jnp.stack([first, 2 * nc - 1 - first]).astype(jnp.int32)
    blocks = jnp.stack([pairing, 2 * nc - 1 - pairing], axis=1).reshape(-1).astype(jnp.int32)

    picks = (buckets[::-1][None, :] == jnp.arange(nbuckets, dtype=jnp.int32)[:, None]).astype(BF)
    bias = jnp.dot(table.T, picks, preferred_element_type=F32).reshape(pairs, 2, seq_len)

    rows_in = tokens[0].astype(F32)
    incoming = cotangent[0]
    a_one_full, norm_one_back = jax.vjp(norm_apply, rows_in, g_one)
    a_one = a_one_full.astype(BF)
    a_one_all = norm_apply(tokens_all.astype(F32), g_one).astype(BF)
    query = product(a_one, w_q).astype(BF)
    kv = product(a_one_all, w_kv).astype(BF)
    cross_kv = product(states_all, c_kv).astype(BF)
    attended, self_probs = self_forward(blocks, own, query, kv, bias)
    second = rows_in + product(attended, w_o)
    a_two, norm_two_back = jax.vjp(norm_apply, second, g_two)
    a_two = a_two.astype(BF)
    cross_q = product(a_two, c_q).astype(BF)
    cross_o, cross_probs = cross_forward(cross_q, cross_kv)
    third = second + product(cross_o, c_o)
    a_three, norm_three_back = jax.vjp(norm_apply, third, g_three)
    a_three = a_three.astype(BF)
    gate = product(a_three, w_gate)
    up_val = product(a_three, w_up)
    hidden, geglu_back = jax.vjp(lambda left, right: jax.nn.gelu(left, approximate=True) * right, gate, up_val)
    hidden = hidden.astype(BF)
    result = third + product(hidden, w_down)

    grad_hidden = through(incoming, w_down)
    grad_down = weight_grad(hidden, incoming)
    grad_gate, grad_up = geglu_back(grad_hidden)
    grad_gate = grad_gate.astype(BF)
    grad_up = grad_up.astype(BF)
    grad_w_gate = weight_grad(a_three, grad_gate).astype(BF)
    grad_w_up = weight_grad(a_three, grad_up).astype(BF)
    total_down = net.reduce_weights(grad_down.astype(BF)).astype(F32)
    total_ff = net.reduce_weights(jnp.concatenate([grad_w_gate, grad_w_up], axis=1)).astype(F32)
    grad_a_three = through(grad_gate, w_gate) + through(grad_up, w_up)
    part_three, grad_g_three = norm_three_back(grad_a_three)
    grad_third = incoming.astype(F32) + part_three
    branch_two = grad_third.astype(BF)
    grad_c_o = weight_grad(cross_o, branch_two)
    grad_cross_o = through(branch_two, c_o).astype(BF)
    dcq, dck, dcv = cross_backward(cross_q, cross_kv, grad_cross_o, cross_probs)
    grad_c_q = weight_grad(a_two, dcq)
    grad_c_k = weight_grad(states_all, dck)
    grad_c_v = weight_grad(states_all, dcv)
    states_part = through(dck, c_kv[:, :width]) + through(dcv, c_kv[:, width:])
    part_two, grad_g_two = norm_two_back(through(dcq, c_q))
    grad_second = grad_third + part_two
    branch_one = grad_second.astype(BF)
    grad_w_o = weight_grad(attended, branch_one)
    total_two = net.reduce_weights(
        jnp.concatenate([g.astype(BF) for g in (grad_w_o, grad_c_q, grad_c_k, grad_c_v, grad_c_o)], axis=1)
    ).astype(F32)
    grad_attended = through(branch_one, w_o).astype(BF)
    dq, dk, dv, bias_grad = self_backward(blocks, own, query, kv, grad_attended, self_probs)
    table_grad = lax.dot_general(
        picks.astype(F32), bias_grad.reshape(heads, seq_len), LAST, precision=lax.Precision.HIGHEST
    )
    grad_w_q = weight_grad(a_one, dq)
    grad_w_k = weight_grad(a_one_all, dk)
    grad_w_v = weight_grad(a_one_all, dv)
    rows_part = through(dk, w_kv[:, :width]) + through(dv, w_kv[:, width:])
    sent = jnp.concatenate(
        [rows_part.astype(BF).reshape(nc, count, width), states_part.astype(BF).reshape(nc, -1, width)], axis=1
    )
    own_part = net.scatter_ctx(sent)
    grad_a_one = through(dq, w_q) + own_part[:count]
    grad_states = own_part[count:]
    part_one, grad_g_one = norm_one_back(grad_a_one)
    grad_rows = grad_second + part_one

    small_grad = jnp.stack([grad_g_one, grad_g_two, grad_g_three], axis=1).astype(BF)
    small_grad = jnp.pad(small_grad, ((0, 0), (0, extra_width - 3)))
    table_rows = jnp.pad(
        table_grad.astype(BF).reshape(nz, 1, table_size),
        ((0, 0), (0, shard - 1), (4, extra_width - 4 - table_size)),
    ).reshape(nz * shard, extra_width)
    total_one = net.reduce_weights(
        jnp.concatenate(
            [grad_w_q.astype(BF), grad_w_k.astype(BF), grad_w_v.astype(BF), small_grad + table_rows], axis=1
        )
    ).astype(F32)
    small_total = total_one[:, 3 * width :]
    gain_total = small_total[:, :4].T
    table_total = small_total[0, 4 : 4 + table_size].reshape(-1, heads)

    return (
        result.astype(BF)[None],
        grad_rows[None],
        grad_states[None],
        gain_total[0],
        total_one[:, :width],
        total_one[:, width : 2 * width],
        total_one[:, 2 * width : 3 * width],
        total_two[:, :width],
        table_total,
        gain_total[1],
        total_two[:, width : 2 * width],
        total_two[:, 2 * width : 3 * width],
        total_two[:, 3 * width : 4 * width],
        total_two[:, 4 * width :],
        gain_total[2],
        total_ff[:, :hidden_width],
        total_ff[:, hidden_width:],
        total_down,
    )


def solution(mesh):
    rows = P("fsdp", "ctx", None)
    gain = P("fsdp")
    weight = P("fsdp", None)
    gradients = (
        gain, weight, weight, weight, weight, weight, gain, weight, weight, weight, weight, gain, weight, weight, weight
    )
    return jax.shard_map(
        per_device,
        mesh=mesh,
        in_specs=(rows, rows, rows, P(), P()) + gradients,
        out_specs=(rows, rows, rows) + gradients,
        check_vma=False,
    )
```

time: 1430 us -> 551 us (0.39)
  local copies, waits for them, and re-layouts: 579 us -> 84.1 us
  waiting for transfers between devices: 600 us -> 258 us
  blocking collectives: 75.6 us -> 0 us
  starting transfers between devices: 1.17 us -> 61.9 us
  matrix products: 116 us -> 61.5 us
  Pallas kernels: 0 us -> 29 us
    gather x2 -> x0, local copies, waits for them, and re-layouts: 521 us -> none  [pair_buckets(): bucket_ids = jnp.take(buckets, spots)]
    reduce_scatter x9 -> x0, waiting for transfers between devices: 367 us -> none  [the longest x1 62.6 us: per_device(): lax.psum_scatter(grad_down.astype(jnp.bfloat16), 'fsdp', scatter_dimensio...]
    ppermute x0 -> x66, waiting for transfers between devices: none -> 195 us  [the longest x36 155 us: to_chip(): return lax.ppermute(x, 'ctx', [(i, i ^ 2 * k) for i in range(self.nc)])]
    unnamed x35 -> x3, waiting for transfers between devices: 137 us -> 0.05 us
    ppermute x0 -> x66, starting transfers between devices: none -> 61.8 us  [the longest x36 33.6 us: to_chip(): return lax.ppermute(x, 'ctx', [(i, i ^ 2 * k) for i in range(self.nc)])]
    dot_general x47 -> x33, matrix products: 116 us -> 61.5 us  [the longest x11 22.6 us: weight_grad(): return lax.dot_general(a, grad, FIRST, preferred_element_type=F32)]
    psum x1 -> x0, waiting for transfers between devices: 54.3 us -> none  [per_device(): lax.psum(shards[8].astype(jnp.bfloat16), 'ctx').astype(jnp.float32)]
    all_gather x3 -> x0, blocking collectives: 33.9 us -> none  [the longest x1 14.1 us: per_device(): lax.all_gather(key_part, 'ctx', axis=0, tiled=True)]
  transfers between devices with their start and end apart: 29 -> 69, of which waited for: 18 -> 28; matrix products, arithmetic and copies ran while one was open for 48% -> 24% of each run, Pallas kernels for 0% -> 2%
where the time goes in v1:
time: 551 us; the launch traced here: 546 us
  waiting for transfers between devices  258 us (47%)
  local copies, waits for them, and re-layouts  84.1 us (15%)
  starting transfers between devices  61.9 us (11%)
  matrix products  61.5 us (11%)
  other arithmetic  34.8 us (6%)
  Pallas kernels  29 us (5%)
  between operations  16.9 us (3%)
    ppermute x36, waiting for transfers between devices, to_chip(): return lax.ppermute(x, 'ctx', [(i, i ^ 2 * k) for i in range(self.nc)])  155 us
    all_gather x1, waiting for transfers between devices, per_device(): lax.all_gather(rows_of(ff_down), ('fsdp', 'ctx'), axis=0, tiled=True)  57.7 us
    ppermute x18, waiting for transfers between devices, along(): return lax.ppermute(x, 'fsdp', [(i, (i + s) % n) for i in range(n)])  39.2 us
    ppermute x36, starting transfers between devices, to_chip(): return lax.ppermute(x, 'ctx', [(i, i ^ 2 * k) for i in range(self.nc)])  33.6 us
    dot_general x11, matrix products, weight_grad(): return lax.dot_general(a, grad, FIRST, preferred_element_type=F32)  22.6 us
    dot_general x11, matrix products, through(): return lax.dot_general(grad, w, LAST, preferred_element_type=F32)  21.6 us
    ppermute x18, starting transfers between devices, along(): return lax.ppermute(x, 'fsdp', [(i, (i + s) % n) for i in range(n)])  19.1 us
    dot_general x9, matrix products, product(): return jnp.dot(a, w, preferred_element_type=F32)  17 us
  transfers between devices with their start and end apart: 69, of which 28 were waited for; matrix products, arithmetic and copies ran while one was open for 24% of the time, Pallas kernels for 2%

profile of v1, /device:TPU:1, one launch (start us, length us, event | category | flops | bytes accessed | tf_op | source)
XLA Modules:
  0.0 546.1 jit_solution(4487109700104504427)
XLA Ops:
  34.5 5.6 %collective-permute-done.11 = bf16[24,3840]{1,0:T(8,128)(2,1)S(1)} collective-permute-done((bf16[24,3840]{1,0:T(8,128)(2,1)S(1)}, bf16[24,3840]{1,0:T(8,128)(2,1)S(1)}, u32[]{:S(2)}, u32[]{:S(2)}) %collective-permute-start.11) | collective-permute-done | bytes 184352 | tf_op jit(solution)/shard_map/ppermute | solution.py:301
  40.4 8.8 %collective-permute-done.12 = bf16[24,3840]{1,0:T(8,128)(2,1)S(1)} collective-permute-done((bf16[24,3840]{1,0:T(8,128)(2,1)S(1)}, bf16[24,3840]{1,0:T(8,128)(2,1)S(1)}, u32[]{:S(2)}, u32[]{:S(2)}) %collective-permute-start.12) | collective-permute-done | bytes 184352 | tf_op jit(solution)/shard_map/ppermute | solution.py:301
  55.6 6.9 %collective-permute-done.5 = bf16[4,24,2432]{2,1,0:T(8,128)(2,1)S(1)} collective-permute-done((bf16[4,24,2432]{2,1,0:T(8,128)(2,1)S(1)}, bf16[4,24,2432]{2,1,0:T(8,128)(2,1)S(1)}, u32[]{:S(2)}, u32[]{:S(2)}) %collective-permute-start.5) | collective-permute-done | bytes 466976 | tf_op jit(solution)/shard_map/ppermute | solution.py:297
  62.5 17.7 %collective-permute-done.4 = bf16[4,24,2432]{2,1,0:T(8,128)(2,1)S(1)} collective-permute-done((bf16[4,24,2432]{2,1,0:T(8,128)(2,1)S(1)}, bf16[4,24,2432]{2,1,0:T(8,128)(2,1)S(1)}, u32[]{:S(2)}, u32[]{:S(2)}) %collective-permute-start.4) | collective-permute-done | bytes 466976 | tf_op jit(solution)/shard_map/ppermute | solution.py:297
  81.8 12.1 %collective-permute-done.16 = bf16[4,24,3840]{2,1,0:T(8,128)(2,1)S(1)} collective-permute-done((bf16[4,24,3840]{2,1,0:T(8,128)(2,1)S(1)}, bf16[4,24,3840]{2,1,0:T(8,128)(2,1)S(1)}, u32[]{:S(2)}, u32[]{:S(2)}) %collective-permute-start.16) | collective-permute-done | bytes 737312 | tf_op jit(solution)/shard_map/ppermute | solution.py:297
  93.9 16.8 %collective-permute-done.15 = bf16[4,24,3840]{2,1,0:T(8,128)(2,1)S(1)} collective-permute-done((bf16[4,24,3840]{2,1,0:T(8,128)(2,1)S(1)}, bf16[4,24,3840]{2,1,0:T(8,128)(2,1)S(1)}, u32[]{:S(2)}, u32[]{:S(2)}) %collective-permute-start.15) | collective-permute-done | bytes 737312 | tf_op jit(solution)/shard_map/ppermute | solution.py:297
  125.4 4.1 convolution_convert_fusion.k_ref.v_ref
  129.5 9.2 %self_forward.1 = (bf16[128,768]{1,0:T(8,128)(2,1)S(1)}, bf16[6,256,1024]{2,1,0:T(8,128)(2,1)S(1)}) custom-call(s32[16]{0:T(128)S(1)} %reshape.220.blocks_ref, s32[2]{0:T(128)S(1)} %pad_add_fusion.2.own_ref, bf16[128,768]{1,0:T(8,128)(2,1)S(1)} %convolution_convert_fusion.16.q_ref, bf16[1024,1536]{1,0:T(8,128)(2,1)} %convolution_convert_fusion.k_ref.v_ref, ...), custom_call_target="tpu_custom_call" | custom-call | flops 805306368 | bytes 9437184 | tf_op jit(solution)/shard_map/self_forward/pallas_call | solution.py:174
  147.8 4.4 cross_forward.1
  154.5 3.6 fusion.113
  158.1 4.9 all-gather.6.cloned.1.call-done
  166.5 57.7 %all-gather.8.cloned.1.call-done = bf16[2048,768]{1,0:T(8,128)(2,1)} async-done(((bf16[64,768]{1,0:T(8,128)(2,1)}), bf16[2048,768]{1,0:T(8,128)(2,1)}) %all-gather.8.cloned.1.call-update) | async-done | bytes 3145744 | tf_op jit(solution)/shard_map/all_gather | solution.py:401
  224.2 5.0 multiply_convert_fusion
  235.5 4.7 cross_backward.1
  241.7 10.7 %self_backward.1 = (bf16[128,768]{1,0:T(8,128)(2,1)S(1)}, bf16[1024,768]{1,0:T(8,128)(2,1)S(1)}, bf16[1024,768]{1,0:T(8,128)(2,1)S(1)}, f32[6,2,1024]{2,1,0:T(2,128)S(1)}) custom-call(s32[16]{0:T(128)S(1)} %reshape.220.blocks_ref, s32[2]{0:T(128)S(1)} %pad_add_fusion.2.own_ref, bf16[128,768]{1,0:T(8,128)(2,1)S(1)} %copy-done.4, ...), custom_call_target="tpu_custom_call" | custom-call | flops 2013265920 | bytes 9437184 | tf_op jit(solution)/shard_map/self_backward/pallas_call | solution.py:202
  284.2 8.7 %copy.75 = bf16[768,3840]{1,0:T(8,128)(2,1)} copy(bf16[768,3840]{0,1:T(8,128)(2,1)} %fusion.12) | data formatting | bytes 11796480 | tf_op jit(solution)/shard_map/concatenate | solution.py:477
  293.0 3.8 dynamic-slice_bitcast_fusion
  311.7 5.4 collective-permute-done.21
  318.8 5.1 collective-permute-done.20
  336.5 6.1 %copy.74 = bf16[768,2432]{1,0:T(8,128)(2,1)} copy(bf16[768,2432]{0,1:T(8,128)(2,1)} %pad_maximum_fusion.1) | data formatting | bytes 7471104 | tf_op jit(solution)/shard_map/concatenate | solution.py:504
  343.1 9.3 %collective-permute-done.57 = bf16[4,64,768]{2,1,0:T(8,128)(2,1)} collective-permute-done((bf16[4,64,768]{2,1,0:T(8,128)(2,1)}, bf16[4,64,768]{2,1,0:T(8,128)(2,1)}, u32[]{:S(2)}, u32[]{:S(2)}) %collective-permute-start.57) | collective-permute-done | bytes 393248 | tf_op jit(solution)/shard_map/ppermute | solution.py:297
  358.2 7.3 %collective-permute-done.60 = bf16[64,768]{1,0:T(8,128)(2,1)S(1)} collective-permute-done((bf16[64,768]{1,0:T(8,128)(2,1)S(1)}, bf16[64,768]{1,0:T(8,128)(2,1)S(1)}, u32[]{:S(2)}, u32[]{:S(2)}) %collective-permute-start.60) | collective-permute-done | bytes 98336 | tf_op jit(solution)/shard_map/ppermute | solution.py:301
  389.6 9.8 %collective-permute-done.36 = bf16[4,24,3840]{2,1,0:T(8,128)(2,1)S(1)} collective-permute-done((bf16[4,24,3840]{2,1,0:T(8,128)(2,1)S(1)}, bf16[4,24,3840]{2,1,0:T(8,128)(2,1)S(1)}, u32[]{:S(2)}, u32[]{:S(2)}) %collective-permute-start.36) | collective-permute-done | bytes 737312 | tf_op jit(solution)/shard_map/ppermute | solution.py:297
  400.5 16.1 %collective-permute-done.35 = bf16[4,24,3840]{2,1,0:T(8,128)(2,1)S(1)} collective-permute-done((bf16[4,24,3840]{2,1,0:T(8,128)(2,1)S(1)}, bf16[4,24,3840]{2,1,0:T(8,128)(2,1)S(1)}, u32[]{:S(2)}, u32[]{:S(2)}) %collective-permute-start.35) | collective-permute-done | bytes 737312 | tf_op jit(solution)/shard_map/ppermute | solution.py:297
  419.0 6.3 %collective-permute-done.25 = bf16[4,24,2432]{2,1,0:T(8,128)(2,1)S(1)} collective-permute-done((bf16[4,24,2432]{2,1,0:T(8,128)(2,1)S(1)}, bf16[4,24,2432]{2,1,0:T(8,128)(2,1)S(1)}, u32[]{:S(2)}, u32[]{:S(2)}) %collective-permute-start.25) | collective-permute-done | bytes 466976 | tf_op jit(solution)/shard_map/ppermute | solution.py:297
  425.3 10.7 %collective-permute-done.24 = bf16[4,24,2432]{2,1,0:T(8,128)(2,1)S(1)} collective-permute-done((bf16[4,24,2432]{2,1,0:T(8,128)(2,1)S(1)}, bf16[4,24,2432]{2,1,0:T(8,128)(2,1)S(1)}, u32[]{:S(2)}, u32[]{:S(2)}) %collective-permute-start.24) | collective-permute-done | bytes 466976 | tf_op jit(solution)/shard_map/ppermute | solution.py:297
  444.7 5.7 %collective-permute-done.27 = bf16[24,2432]{1,0:T(8,128)(2,1)S(1)} collective-permute-done((bf16[24,2432]{1,0:T(8,128)(2,1)S(1)}, bf16[24,2432]{1,0:T(8,128)(2,1)S(1)}, u32[]{:S(2)}, u32[]{:S(2)}) %collective-permute-start.27) | collective-permute-done | bytes 116768 | tf_op jit(solution)/shard_map/ppermute | solution.py:301
  452.7 3.8 collective-permute-done.47
  457.8 18.1 %collective-permute-done.46 = bf16[4,24,4096]{2,1,0:T(8,128)(2,1)S(1)} collective-permute-done((bf16[4,24,4096]{2,1,0:T(8,128)(2,1)S(1)}, bf16[4,24,4096]{2,1,0:T(8,128)(2,1)S(1)}, u32[]{:S(2)}, u32[]{:S(2)}) %collective-permute-start.46) | collective-permute-done | bytes 786464 | tf_op jit(solution)/shard_map/ppermute | solution.py:297
  482.3 5.2 collective-permute-done.30
  491.4 11.8 %collective-permute-done.49 = bf16[24,4096]{1,0:T(8,128)(2,1)S(1)} collective-permute-done((bf16[24,4096]{1,0:T(8,128)(2,1)S(1)}, bf16[24,4096]{1,0:T(8,128)(2,1)S(1)}, u32[]{:S(2)}, u32[]{:S(2)}) %collective-permute-start.49) | collective-permute-done | bytes 196640 | tf_op jit(solution)/shard_map/ppermute | solution.py:301
  512.0 4.5 collective-permute-done.52
  (547 shorter events, 219.4 us)
Async XLA Ops:
  7.2 147.3 %all-gather.4.cloned.1.call-start = ((), (), s32[]{:S(2)}) async-start(), calls=%async_computation | async-start | bytes 3244032 | tf_op jit(solution)/shard_map/all_gather | solution.py:399
  9.0 153.9 %all-gather.6.cloned.1.call-start = ((), (), s32[]{:S(2)}) async-start(), calls=%async_computation.1 | async-start | bytes 3244032 | tf_op jit(solution)/shard_map/all_gather | solution.py:400
  10.6 213.5 %all-gather.8.cloned.1.call-start = ((), (), s32[]{:S(2)}) async-start(), calls=%async_computation.2 | async-start | bytes 3244032 | tf_op jit(solution)/shard_map/all_gather | solution.py:401
  21.8 30.0 %collective-permute-start.9 = (bf16[192,768]{1,0:T(8,128)(2,1)S(1)}, bf16[192,768]{1,0:T(8,128)(2,1)S(1)}, u32[]{:S(2)}, u32[]{:S(2)}) collective-permute-start(bf16[192,768]{1,0:T(8,128)(2,1)S(1)} %get-tuple-element.105), channel_id=1, source_target_pairs={{0,24},{4,28},{8,16},{12,20},{16,8},{20,12},{24,0},{28,4},{1,25},{... | collective-permute-start | bytes 884744 | tf_op jit(solution)/shard_map/ppermute | solution.py:297
  24.0 28.0 %collective-permute-start.8 = (bf16[192,768]{1,0:T(8,128)(2,1)S(1)}, bf16[192,768]{1,0:T(8,128)(2,1)}, u32[]{:S(2)}, u32[]{:S(2)}) collective-permute-start(bf16[192,768]{1,0:T(8,128)(2,1)S(1)} %get-tuple-element.105), channel_id=1, source_target_pairs={{0,16},{4,20},{8,24},{12,28},{16,0},{20,4},{24,8},{28,12},{1,17},{... | collective-permute-start | bytes 884744 | tf_op jit(solution)/shard_map/ppermute | solution.py:297
  33.2 21.2 %collective-permute-start.7 = (bf16[192,768]{1,0:T(8,128)(2,1)S(1)}, bf16[192,768]{1,0:T(8,128)(2,1)S(1)}, u32[]{:S(2)}, u32[]{:S(2)}) collective-permute-start(bf16[192,768]{1,0:T(8,128)(2,1)S(1)} %get-tuple-element.105), channel_id=1, source_target_pairs={{0,8},{4,12},{8,0},{12,4},{16,24},{20,28},{24,16},{28,20},{1,9},{5... | collective-permute-start | bytes 884744 | tf_op jit(solution)/shard_map/ppermute | solution.py:297
  51.5 28.7 %collective-permute-start.4 = (bf16[4,24,2432]{2,1,0:T(8,128)(2,1)S(1)}, bf16[4,24,2432]{2,1,0:T(8,128)(2,1)S(1)}, u32[]{:S(2)}, u32[]{:S(2)}) collective-permute-start(bf16[4,24,2432]{2,1,0:T(8,128)(2,1)S(1)} %bitcast_dynamic-update-slice_fusion.4), channel_id=1, source_target_pairs={{0,16},{4,20},{8,24},{12,28},{16,0},{20,4},{24,8},{28,12},{1,17},{... | collective-permute-start | bytes 1400840 | tf_op jit(solution)/shard_map/ppermute | solution.py:297
  51.8 29.7 %collective-permute-start.3 = (bf16[4,24,2432]{2,1,0:T(8,128)(2,1)S(1)}, bf16[4,24,2432]{2,1,0:T(8,128)(2,1)S(1)}, u32[]{:S(2)}, u32[]{:S(2)}) collective-permute-start(bf16[4,24,2432]{2,1,0:T(8,128)(2,1)S(1)} %bitcast_dynamic-update-slice_fusion.4), channel_id=1, source_target_pairs={{0,8},{4,12},{8,0},{12,4},{16,24},{20,28},{24,16},{28,20},{1,9},{5... | collective-permute-start | bytes 1400840 | tf_op jit(solution)/shard_map/ppermute | solution.py:297
  52.1 41.9 %collective-permute-start.16 = (bf16[4,24,3840]{2,1,0:T(8,128)(2,1)S(1)}, bf16[4,24,3840]{2,1,0:T(8,128)(2,1)S(1)}, u32[]{:S(2)}, u32[]{:S(2)}) collective-permute-start(bf16[4,24,3840]{2,1,0:T(8,128)(2,1)S(1)} %bitcast_dynamic-update-slice_fusion), channel_id=1, source_target_pairs={{0,24},{4,28},{8,16},{12,20},{16,8},{20,12},{24,0},{28,4},{1,25},{... | collective-permute-start | bytes 2211848 | tf_op jit(solution)/shard_map/ppermute | solution.py:297
  54.4 56.4 %collective-permute-start.15 = (bf16[4,24,3840]{2,1,0:T(8,128)(2,1)S(1)}, bf16[4,24,3840]{2,1,0:T(8,128)(2,1)S(1)}, u32[]{:S(2)}, u32[]{:S(2)}) collective-permute-start(bf16[4,24,3840]{2,1,0:T(8,128)(2,1)S(1)} %bitcast_dynamic-update-slice_fusion), channel_id=1, source_target_pairs={{0,16},{4,20},{8,24},{12,28},{16,0},{20,4},{24,8},{28,12},{1,17},{... | collective-permute-start | bytes 2211848 | tf_op jit(solution)/shard_map/ppermute | solution.py:297
  62.5 48.3 %collective-permute-start.14 = (bf16[4,24,3840]{2,1,0:T(8,128)(2,1)S(1)}, bf16[4,24,3840]{2,1,0:T(8,128)(2,1)S(1)}, u32[]{:S(2)}, u32[]{:S(2)}) collective-permute-start(bf16[4,24,3840]{2,1,0:T(8,128)(2,1)S(1)} %bitcast_dynamic-update-slice_fusion), channel_id=1, source_target_pairs={{0,8},{4,12},{8,0},{12,4},{16,24},{20,28},{24,16},{28,20},{1,9},{5... | collective-permute-start | bytes 2211848 | tf_op jit(solution)/shard_map/ppermute | solution.py:297
  80.2 33.1 %collective-permute-start.10 = (bf16[4,192,768]{2,1,0:T(8,128)(2,1)S(1)}, bf16[4,192,768]{2,1,0:T(8,128)(2,1)S(1)}, u32[]{:S(2)}, u32[]{:S(2)}) collective-permute-start(bf16[4,192,768]{2,1,0:T(8,128)(2,1)S(1)} %pad_maximum_fusion.4), channel_id=1, source_target_pairs={{0,4},{4,0},{8,12},{12,8},{16,20},{20,16},{24,28},{28,24},{1,5},{5... | collective-permute-start | bytes 3538952 | tf_op jit(solution)/shard_map/ppermute | solution.py:294
  81.8 35.0 %collective-permute-start.6 = (bf16[4,4,24,2432]{3,2,0,1:T(8,128)(2,1)S(1)}, bf16[4,4,24,2432]{3,2,0,1:T(8,128)(2,1)S(1)}, u32[]{:S(2)}, u32[]{:S(2)}) collective-permute-start(bf16[4,4,24,2432]{3,2,0,1:T(8,128)(2,1)S(1)} %pad_maximum_fusion.3), channel_id=1, source_target_pairs={{0,4},{4,0},{8,12},{12,8},{16,20},{20,16},{24,28},{28,24},{1,5},{5... | collective-permute-start | bytes 5603336 | tf_op jit(solution)/shard_map/ppermute | solution.py:294
  112.9 25.9 %collective-permute-start.17 = (bf16[4,4,24,3840]{3,2,0,1:T(8,128)(2,1)}, bf16[4,4,24,3840]{3,2,0,1:T(8,128)(2,1)}, u32[]{:S(2)}, u32[]{:S(2)}) collective-permute-start(bf16[4,4,24,3840]{3,2,0,1:T(8,128)(2,1)} %pad_maximum_fusion.2), channel_id=1, source_target_pairs={{0,4},{4,0},{8,12},{12,8},{16,20},{20,16},{24,28},{28,24},{1,5},{5... | collective-permute-start | bytes 8847368 | tf_op jit(solution)/shard_map/ppermute | solution.py:294
  272.9 32.6 %collective-permute-start.18 = (bf16[4,192,768]{2,1,0:T(8,128)(2,1)}, bf16[4,192,768]{2,1,0:T(8,128)(2,1)}, u32[]{:S(2)}, u32[]{:S(2)}) collective-permute-start(bf16[4,192,768]{2,1,0:T(8,128)(2,1)} %fusion.21), channel_id=1, source_target_pairs={{0,4},{4,0},{8,12},{12,8},{16,20},{20,16},{24,28},{28,24},{1,5},{5... | collective-permute-start | bytes 3538952 | tf_op jit(solution)/shard_map/ppermute | solution.py:294
  296.8 81.1 %collective-permute-start.33 = (bf16[4,4,24,3840]{3,2,0,1:T(8,128)(2,1)}, bf16[4,4,24,3840]{3,2,0,1:T(8,128)(2,1)}, u32[]{:S(2)}, u32[]{:S(2)}) collective-permute-start(bf16[4,4,24,3840]{3,2,0,1:T(8,128)(2,1)} %dynamic-slice_bitcast_fusion), channel_id=1, source_target_pairs={{0,4},{4,0},{8,12},{12,8},{16,20},{20,16},{24,28},{28,24},{1,5},{5... | collective-permute-start | bytes 8847368 | tf_op jit(solution)/shard_map/ppermute | solution.py:294
  300.7 26.7 %collective-permute-start.55 = (bf16[4,4,64,768]{3,2,1,0:T(8,128)(2,1)}, bf16[4,4,64,768]{3,2,1,0:T(8,128)(2,1)}, u32[]{:S(2)}, u32[]{:S(2)}) collective-permute-start(bf16[4,4,64,768]{3,2,1,0:T(8,128)(2,1)} %bitcast.346), channel_id=1, source_target_pairs={{0,4},{4,0},{8,12},{12,8},{16,20},{20,16},{24,28},{28,24},{1,5},{5... | collective-permute-start | bytes 4718600 | tf_op jit(solution)/shard_map/ppermute | solution.py:294
  317.1 66.4 %collective-permute-start.44 = (bf16[4,4,24,4096]{3,2,1,0:T(8,128)(2,1)}, bf16[4,4,24,4096]{3,2,1,0:T(8,128)(2,1)}, u32[]{:S(2)}, u32[]{:S(2)}) collective-permute-start(bf16[4,4,24,4096]{3,2,1,0:T(8,128)(2,1)} %bitcast.345), channel_id=1, source_target_pairs={{0,4},{4,0},{8,12},{12,8},{16,20},{20,16},{24,28},{28,24},{1,5},{5... | collective-permute-start | bytes 9437192 | tf_op jit(solution)/shard_map/ppermute | solution.py:294
  332.9 19.5 %collective-permute-start.57 = (bf16[4,64,768]{2,1,0:T(8,128)(2,1)}, bf16[4,64,768]{2,1,0:T(8,128)(2,1)}, u32[]{:S(2)}, u32[]{:S(2)}) collective-permute-start(bf16[4,64,768]{2,1,0:T(8,128)(2,1)} %get-tuple-element.88), channel_id=1, source_target_pairs={{0,16},{4,20},{8,24},{12,28},{16,0},{20,4},{24,8},{28,12},{1,17},{... | collective-permute-start | bytes 1179656 | tf_op jit(solution)/shard_map/ppermute | solution.py:297
  382.0 34.6 %collective-permute-start.35 = (bf16[4,24,3840]{2,1,0:T(8,128)(2,1)S(1)}, bf16[4,24,3840]{2,1,0:T(8,128)(2,1)S(1)}, u32[]{:S(2)}, u32[]{:S(2)}) collective-permute-start(bf16[4,24,3840]{2,1,0:T(8,128)(2,1)S(1)} %get-tuple-element.76), channel_id=1, source_target_pairs={{0,16},{4,20},{8,24},{12,28},{16,0},{20,4},{24,8},{28,12},{1,17},{... | collective-permute-start | bytes 2211848 | tf_op jit(solution)/shard_map/ppermute | solution.py:297
  383.0 33.6 %collective-permute-start.34 = (bf16[4,24,3840]{2,1,0:T(8,128)(2,1)S(1)}, bf16[4,24,3840]{2,1,0:T(8,128)(2,1)S(1)}, u32[]{:S(2)}, u32[]{:S(2)}) collective-permute-start(bf16[4,24,3840]{2,1,0:T(8,128)(2,1)S(1)} %get-tuple-element.74), channel_id=1, source_target_pairs={{0,8},{4,12},{8,0},{12,4},{16,24},{20,28},{24,16},{28,20},{1,9},{5... | collective-permute-start | bytes 2211848 | tf_op jit(solution)/shard_map/ppermute | solution.py:297
  387.3 38.0 %collective-permute-start.25 = (bf16[4,24,2432]{2,1,0:T(8,128)(2,1)S(1)}, bf16[4,24,2432]{2,1,0:T(8,128)(2,1)S(1)}, u32[]{:S(2)}, u32[]{:S(2)}) collective-permute-start(bf16[4,24,2432]{2,1,0:T(8,128)(2,1)S(1)} %get-tuple-element.84), channel_id=1, source_target_pairs={{0,24},{4,28},{8,16},{12,20},{16,8},{20,12},{24,0},{28,4},{1,25},{... | collective-permute-start | bytes 1400840 | tf_op jit(solution)/shard_map/ppermute | solution.py:297
  388.6 47.4 %collective-permute-start.24 = (bf16[4,24,2432]{2,1,0:T(8,128)(2,1)S(1)}, bf16[4,24,2432]{2,1,0:T(8,128)(2,1)S(1)}, u32[]{:S(2)}, u32[]{:S(2)}) collective-permute-start(bf16[4,24,2432]{2,1,0:T(8,128)(2,1)S(1)} %get-tuple-element.85), channel_id=1, source_target_pairs={{0,16},{4,20},{8,24},{12,28},{16,0},{20,4},{24,8},{28,12},{1,17},{... | collective-permute-start | bytes 1400840 | tf_op jit(solution)/shard_map/ppermute | solution.py:297
  399.4 36.5 %collective-permute-start.23 = (bf16[4,24,2432]{2,1,0:T(8,128)(2,1)S(1)}, bf16[4,24,2432]{2,1,0:T(8,128)(2,1)S(1)}, u32[]{:S(2)}, u32[]{:S(2)}) collective-permute-start(bf16[4,24,2432]{2,1,0:T(8,128)(2,1)S(1)} %get-tuple-element.83), channel_id=1, source_target_pairs={{0,8},{4,12},{8,0},{12,4},{16,24},{20,28},{24,16},{28,20},{1,9},{5... | collective-permute-start | bytes 1400840 | tf_op jit(solution)/shard_map/ppermute | solution.py:297
  417.0 21.5 %collective-permute-start.39 = (bf16[24,3840]{1,0:T(8,128)(2,1)S(1)}, bf16[24,3840]{1,0:T(8,128)(2,1)S(1)}, u32[]{:S(2)}, u32[]{:S(2)}) collective-permute-start(bf16[24,3840]{1,0:T(8,128)(2,1)S(1)} %get-tuple-element.96), channel_id=1, source_target_pairs={{0,3},{1,0},{2,1},{3,2},{4,7},{5,4},{6,5},{7,6},{8,11},{9,8},{10,9... | collective-permute-start | bytes 552968 | tf_op jit(solution)/shard_map/ppermute | solution.py:301
  417.8 21.9 %collective-permute-start.38 = (bf16[24,3840]{1,0:T(8,128)(2,1)S(1)}, bf16[24,3840]{1,0:T(8,128)(2,1)S(1)}, u32[]{:S(2)}, u32[]{:S(2)}) collective-permute-start(bf16[24,3840]{1,0:T(8,128)(2,1)S(1)} %get-tuple-element.97), channel_id=1, source_target_pairs={{0,2},{1,3},{2,0},{3,1},{4,6},{5,7},{6,4},{7,5},{8,10},{9,11},{10,... | collective-permute-start | bytes 552968 | tf_op jit(solution)/shard_map/ppermute | solution.py:301
  437.4 19.2 %collective-permute-start.47 = (bf16[4,24,4096]{2,1,0:T(8,128)(2,1)S(1)}, bf16[4,24,4096]{2,1,0:T(8,128)(2,1)S(1)}, u32[]{:S(2)}, u32[]{:S(2)}) collective-permute-start(bf16[4,24,4096]{2,1,0:T(8,128)(2,1)S(1)} %get-tuple-element.67), channel_id=1, source_target_pairs={{0,24},{4,28},{8,16},{12,20},{16,8},{20,12},{24,0},{28,4},{1,25},{... | collective-permute-start | bytes 2359304 | tf_op jit(solution)/shard_map/ppermute | solution.py:297
  438.6 37.3 %collective-permute-start.46 = (bf16[4,24,4096]{2,1,0:T(8,128)(2,1)S(1)}, bf16[4,24,4096]{2,1,0:T(8,128)(2,1)S(1)}, u32[]{:S(2)}, u32[]{:S(2)}) collective-permute-start(bf16[4,24,4096]{2,1,0:T(8,128)(2,1)S(1)} %get-tuple-element.68), channel_id=1, source_target_pairs={{0,16},{4,20},{8,24},{12,28},{16,0},{20,4},{24,8},{28,12},{1,17},{... | collective-permute-start | bytes 2359304 | tf_op jit(solution)/shard_map/ppermute | solution.py:297
  439.7 37.3 %collective-permute-start.45 = (bf16[4,24,4096]{2,1,0:T(8,128)(2,1)S(1)}, bf16[4,24,4096]{2,1,0:T(8,128)(2,1)S(1)}, u32[]{:S(2)}, u32[]{:S(2)}) collective-permute-start(bf16[4,24,4096]{2,1,0:T(8,128)(2,1)S(1)} %get-tuple-element.66), channel_id=1, source_target_pairs={{0,8},{4,12},{8,0},{12,4},{16,24},{20,28},{24,16},{28,20},{1,9},{5... | collective-permute-start | bytes 2359304 | tf_op jit(solution)/shard_map/ppermute | solution.py:297
  450.4 55.3 %collective-permute-start.42 = (bf16[24,3840]{1,0:T(8,128)(2,1)S(1)}, bf16[24,3840]{1,0:T(8,128)(2,1)S(1)}, u32[]{:S(2)}, u32[]{:S(2)}) collective-permute-start(bf16[24,3840]{1,0:T(8,128)(2,1)S(1)} %get-tuple-element.57), channel_id=1, source_target_pairs={{0,24},{4,28},{8,16},{12,20},{16,8},{20,12},{24,0},{28,4},{1,25},{... | collective-permute-start | bytes 552968 | tf_op jit(solution)/shard_map/ppermute | solution.py:297
  451.5 55.3 %collective-permute-start.41 = (bf16[24,3840]{1,0:T(8,128)(2,1)S(1)}, bf16[24,3840]{1,0:T(8,128)(2,1)S(1)}, u32[]{:S(2)}, u32[]{:S(2)}) collective-permute-start(bf16[24,3840]{1,0:T(8,128)(2,1)S(1)} %get-tuple-element.57), channel_id=1, source_target_pairs={{0,16},{4,20},{8,24},{12,28},{16,0},{20,4},{24,8},{28,12},{1,17},{... | collective-permute-start | bytes 552968 | tf_op jit(solution)/shard_map/ppermute | solution.py:297
  456.6 23.3 %collective-permute-start.31 = (bf16[24,2432]{1,0:T(8,128)(2,1)S(1)}, bf16[24,2432]{1,0:T(8,128)(2,1)S(1)}, u32[]{:S(2)}, u32[]{:S(2)}) collective-permute-start(bf16[24,2432]{1,0:T(8,128)(2,1)S(1)} %get-tuple-element.59), channel_id=1, source_target_pairs={{0,24},{4,28},{8,16},{12,20},{16,8},{20,12},{24,0},{28,4},{1,25},{... | collective-permute-start | bytes 350216 | tf_op jit(solution)/shard_map/ppermute | solution.py:297
  (145 other events, 1276.3 us)
Sparse Core Ops, SparseCore 0:
  11.5 90.5 all-gather.3
  105.6 57.3 all-gather.5
  166.4 57.7 all-gather.7

commit v2 on v1

--- a/solution.py
+++ b/solution.py
@@ -280,6 +280,87 @@
     )(q, kv, kv, do, probs)
 
 
+def split_kernel(products, nouts, core_ref, *refs):
+    even = core_ref[0] == 0
+    keep_ref, give_ref = refs[-2:]
+    for i, (half, row, column) in enumerate(products):
+        full = dot(refs[2 * i][...], refs[2 * i + 1][...], FIRST)
+        cols = full.shape[1]
+        for j in range(full.shape[0] // (2 * half)):
+            low = full[2 * j * half : (2 * j + 1) * half]
+            high = full[(2 * j + 1) * half : (2 * j + 2) * half]
+            keep_ref[j, row : row + half, column : column + cols] = jnp.where(even, low, high).astype(BF)
+            give_ref[j, row : row + half, column : column + cols] = jnp.where(even, high, low).astype(BF)
+
+
+def split_grads(core, pairs, places, rows, cols):
+    pieces = pairs[0][0].shape[1] // (2 * places[0][0])
+    shape = jax.ShapeDtypeStruct((pieces, rows, cols), BF)
+    if any(half % 8 != 0 or row % 16 != 0 for half, row, _ in places):
+        keep, give = [], []
+        for (a, g), (half, row, column) in zip(pairs, places):
+            full = weight_grad(a, g).astype(BF).reshape(pieces, 2, half, g.shape[1])
+            spot = ((0, 0), (row, rows - row - half), (column, cols - column - g.shape[1]))
+            keep.append(jnp.pad(lax.dynamic_index_in_dim(full, core, 1, keepdims=False), spot))
+            give.append(jnp.pad(lax.dynamic_index_in_dim(full, 1 - core, 1, keepdims=False), spot))
+        return sum(keep[1:], keep[0]), sum(give[1:], give[0])
+    vmem = pl.BlockSpec(memory_space=pltpu.VMEM)
+    flat = [x for pair in pairs for x in pair]
+    return pl.pallas_call(
+        functools.partial(split_kernel, places, len(places)),
+        in_specs=[pl.BlockSpec(memory_space=pltpu.SMEM)] + [vmem] * len(flat),
+        out_specs=[vmem, vmem],
+        out_shape=[shape, shape],
+        compiler_params=params(),
+        cost_estimate=pl.CostEstimate(
+            flops=sum(2 * a.shape[0] * a.shape[1] * g.shape[1] for a, g in pairs),
+            bytes_accessed=4 * pieces * rows * cols + sum(2 * x.size for x in flat),
+            transcendentals=0,
+        ),
+        name="split_grads",
+    )(core.reshape(1).astype(jnp.int32), *flat)
+
+
+def place_kernel(dims, spot_ref, own_ref, other_ref, gate_ref, up_ref, down_ref):
+    chips, nz, half, wide, down_half = dims
+    for r, ref in enumerate((own_ref, other_ref)):
+        core = spot_ref[1] ^ r
+        for k in range(chips):
+            chip = spot_ref[0] ^ k
+            rows = pl.ds(pl.multiple_of(core * half, half), half)
+            for i, out in enumerate((gate_ref, up_ref)):
+                for z in range(nz):
+                    source = (i * nz + z) * wide
+                    spot = pl.multiple_of((z * chips + chip) * wide, wide)
+                    out[rows, pl.ds(spot, wide)] = ref[k, :half, source : source + wide].astype(F32)
+            rows = pl.ds(pl.multiple_of((2 * chip + core) * down_half, down_half), down_half)
+            down_ref[rows, :] = ref[k, half : half + down_half, : down_ref.shape[1]].astype(F32)
+
+
+def place_ff(chip, core, own, other, nz, half, wide, down_half, width):
+    chips = own.shape[0]
+    hidden = nz * chips * wide
+    shapes = [
+        jax.ShapeDtypeStruct((2 * half, hidden), F32),
+        jax.ShapeDtypeStruct((2 * half, hidden), F32),
+        jax.ShapeDtypeStruct((2 * chips * down_half, width), F32),
+    ]
+    vmem = pl.BlockSpec(memory_space=pltpu.VMEM)
+    return pl.pallas_call(
+        functools.partial(place_kernel, (chips, nz, half, wide, down_half)),
+        in_specs=[pl.BlockSpec(memory_space=pltpu.SMEM), vmem, vmem],
+        out_specs=[vmem] * 3,
+        out_shape=shapes,
+        compiler_params=params(),
+        cost_estimate=pl.CostEstimate(flops=0, bytes_accessed=6 * own.size, transcendentals=0),
+        name="place_ff",
+    )(jnp.stack([chip, core]).astype(jnp.int32), own, other)
+
+
+def fence(*arrays):
+    return lax.optimization_barrier(arrays)
+
+
 class Net:
     def __init__(self):
         self.c = lax.axis_index("ctx")
@@ -300,48 +381,55 @@
         n = self.nz
         return lax.ppermute(x, "fsdp", [(i, (i + s) % n) for i in range(n)])
 
-    def gather_ctx(self, x):
-        got = [x] + [self.to_chip(x, k) for k in range(1, self.chips)]
-        mine = jnp.stack(got)
-        other = self.to_core(mine)
-        out = jnp.zeros((self.nc,) + x.shape, x.dtype)
-        for k in range(self.chips):
-            spot = 2 * (self.chip ^ k)
-            out = lax.dynamic_update_index_in_dim(out, mine[k], spot + self.core, 0)
-            out = lax.dynamic_update_index_in_dim(out, other[k], spot + 1 - self.core, 0)
+
+    def spread_z(self, x):
+        return tuple(self.along(x, s) for s in range(1, self.nz))
+
+    def join_z(self, x, got):
+        out = jnp.zeros((self.nz,) + x.shape, x.dtype)
+        out = lax.dynamic_update_index_in_dim(out, x, self.z, 0)
+        for s, part in enumerate(got, 1):
+            out = lax.dynamic_update_index_in_dim(out, part, (self.z + self.nz - s) % self.nz, 0)
         return out
 
-    def gather_weights(self, piece):
-        rows, cols = piece.shape
-        parts = jnp.zeros((self.nz, rows, cols), piece.dtype)
-        parts = lax.dynamic_update_index_in_dim(parts, piece, self.z, 0)
-        for s in range(1, self.nz):
-            got = self.along(piece, s)
-            parts = lax.dynamic_update_index_in_dim(parts, got, (self.z + self.nz - s) % self.nz, 0)
-        whole = self.gather_ctx(parts)
-        return jnp.swapaxes(whole, 0, 1).reshape(self.nz * self.nc * rows, cols)
-
-    def scatter_ctx(self, x):
-        x = x.reshape((self.chips, 2) + x.shape[1:])
-        keep = lax.dynamic_index_in_dim(x, self.core, 1, keepdims=False)
-        give = lax.dynamic_index_in_dim(x, 1 - self.core, 1, keepdims=False)
-        both = (keep.astype(F32) + self.to_core(give).astype(F32)).astype(BF)
-        total = lax.dynamic_index_in_dim(both, self.chip, 0, keepdims=False).astype(F32)
-        for k in range(1, self.chips):
-            send = lax.dynamic_index_in_dim(both, self.chip ^ k, 0, keepdims=False)
-            total = total + self.to_chip(send, k).astype(F32)
+    def spread_chips(self, x):
+        return tuple(self.to_chip(x, k) for k in range(1, self.chips))
+
+    def join_chips(self, x, got):
+        out = jnp.zeros(x.shape[:1] + (self.chips,) + x.shape[1:], x.dtype)
+        for k, part in enumerate((x,) + tuple(got)):
+            out = lax.dynamic_update_index_in_dim(out, part, self.chip ^ k, 1)
+        return out
+
+    def join_cores(self, x, got):
+        even = self.core == 0
+        return jnp.stack([jnp.where(even, x, got), jnp.where(even, got, x)], axis=2)
+
+
+    def give_chips(self, keep, got):
+        def term(k):
+            spot = self.chip ^ k
+            kept = lax.dynamic_index_in_dim(keep, spot, 1, keepdims=False)
+            other = lax.dynamic_index_in_dim(got, spot, 1, keepdims=False)
+            return (kept.astype(F32) + other.astype(F32)).astype(BF)
+
+        return (term(0),) + tuple(self.to_chip(term(k), k) for k in range(1, self.chips))
+
+    def swap_blocks(self, x):
+        return (x[0],) + tuple(self.to_chip(x[k], k) for k in range(1, self.chips))
+
+    def add(self, parts):
+        total = parts[0].astype(F32)
+        for part in parts[1:]:
+            total = total + part.astype(F32)
         return total
 
-    def reduce_weights(self, grad):
-        rows, cols = grad.shape
-        each = rows // (self.nz * self.nc)
-        x = grad.reshape(self.nz, self.nc, each, cols).swapaxes(0, 1)
-        mine = self.scatter_ctx(x).astype(BF)
-        total = lax.dynamic_index_in_dim(mine, self.z, 0, keepdims=False).astype(F32)
-        for s in range(1, self.nz):
-            send = lax.dynamic_index_in_dim(mine, (self.z + s) % self.nz, 0, keepdims=False)
-            total = total + self.along(send, s).astype(F32)
-        return self.gather_ctx(total.astype(BF)).reshape(self.nc * each, cols)
+    def give_z(self, x):
+        own = lax.dynamic_index_in_dim(x, self.z, 0, keepdims=False)
+        return (own,) + tuple(
+            self.along(lax.dynamic_index_in_dim(x, (self.z + s) % self.nz, 0, keepdims=False), s)
+            for s in range(1, self.nz)
+        )
 
 
 def per_device(
@@ -367,38 +455,65 @@
     ff_down,
 ):
     net = Net()
-    nc, nz = net.nc, net.nz
+    nc, nz, chips = net.nc, net.nz, net.chips
     mine = net.c
     shard = self_query.shape[0]
     width = self_query.shape[1]
-    hidden_width = ff_gate.shape[1]
     heads = bias_table.shape[1]
     pairs = width // LANES
     each = shard // nc
-    down_each = ff_down.shape[0] // nc
+    half = shard // 2
+    down_shard = ff_down.shape[0]
+    wide = down_shard // chips
+    down_half = wide // 2
+    pack_rows = half + down_half
 
     def rows_of(w):
-        n = w.shape[0] // nc
-        return lax.dynamic_slice_in_dim(w, mine * n, n, 0)
+        return lax.dynamic_slice_in_dim(w, mine * each, each, 0)
+
+    def flat(x):
+        return x.reshape(-1, x.shape[-1])
 
     table_size = bias_table.size
     extra_width = LANES * math.ceil((4 + table_size) / LANES)
     small = jnp.stack([norm_one, norm_two, norm_three], axis=1)
     small = jnp.pad(rows_of(small), ((0, 0), (0, extra_width - 3)))
-    flat = jnp.pad(bias_table.reshape(1, -1), ((0, each - 1), (4, extra_width - 4 - table_size)))
-    small = small + flat
-    one = net.gather_weights(
-        jnp.concatenate([rows_of(self_query), rows_of(self_key), rows_of(self_value), small], axis=1)
-    )
-    rows_all = net.gather_ctx(jnp.concatenate([tokens[0], encoder[0]], axis=0))
-    two = net.gather_weights(
-        jnp.concatenate(
-            [rows_of(w) for w in (self_output, cross_query, cross_key, cross_value, cross_output)], axis=1
-        )
-    )
-    w_gate = lax.all_gather(rows_of(ff_gate), ("fsdp", "ctx"), axis=0, tiled=True)
-    w_up = lax.all_gather(rows_of(ff_up), ("fsdp", "ctx"), axis=0, tiled=True)
-    w_down = lax.all_gather(rows_of(ff_down), ("fsdp", "ctx"), axis=0, tiled=True)
+    line = jnp.pad(bias_table.reshape(1, -1), ((0, each - 1), (4, extra_width - 4 - table_size)))
+    one = jnp.concatenate([rows_of(self_query), rows_of(self_key), rows_of(self_value), small + line], axis=1)
+    two = jnp.concatenate(
+        [rows_of(w) for w in (self_output, cross_query, cross_key, cross_value, cross_output)], axis=1
+    )
+
+    def columns_of(w):
+        w = lax.dynamic_slice_in_dim(w, net.core * half, half, 0)
+        return [lax.dynamic_slice_in_dim(w, down_shard * z + wide * net.chip, wide, 1) for z in range(nz)]
+
+    three = jnp.concatenate(columns_of(ff_gate) + columns_of(ff_up), axis=1)
+    pack_cols = max(three.shape[1], width)
+    down = lax.dynamic_slice_in_dim(ff_down, wide * net.chip + down_half * net.core, down_half, 0)
+    three = jnp.concatenate(
+        [
+            jnp.pad(three, ((0, 0), (0, pack_cols - three.shape[1]))),
+            jnp.pad(down, ((0, 0), (0, pack_cols - width))),
+        ],
+        axis=0,
+    )
+    rows_one = jnp.concatenate([tokens[0], encoder[0]], axis=0)
+    incoming = cotangent[0]
+
+    one_z, rows_chips = fence(net.spread_z(one), net.spread_chips(rows_one))
+    one = net.join_z(one, one_z)
+    rows_mine = jnp.stack((rows_one,) + rows_chips)
+    one, rows_mine, two, three = fence(one, rows_mine, two, three)
+    one_chips, rows_core, two_z = fence(net.spread_chips(one), net.to_core(rows_mine), net.spread_z(two))
+    one = net.join_chips(one, one_chips)
+    two = net.join_z(two, two_z)
+    one, two, three, incoming = fence(one, two, three, incoming)
+    one_core = net.to_core(one)
+    three_z = net.spread_z(three)
+    two_chips = net.spread_chips(two)
+    incoming_chips = net.spread_chips(incoming)
+    one = flat(net.join_cores(one, one_core))
 
     w_q = one[:, :width]
     w_kv = one[:, width : 3 * width]
@@ -407,35 +522,40 @@
     g_one, g_two, g_three = gains[0], gains[1], gains[2]
     table = extra.reshape(nz, shard, extra_width)[:, 0, 4 : 4 + table_size].reshape(-1, heads)
     nbuckets = table.shape[0]
-    w_o, c_q, c_kv, c_o = (
-        two[:, :width],
-        two[:, width : 2 * width],
-        two[:, 2 * width : 4 * width],
-        two[:, 4 * width :],
-    )
 
     count = tokens.shape[1]
-    block = count // 2
     seq_len = count * nc
-    tokens_all = rows_all[:, :count].reshape(seq_len, width)
-    states_all = rows_all[:, count:].reshape(-1, width)
-    first = pairing[mine]
-    own = jnp.stack([first, 2 * nc - 1 - first]).astype(jnp.int32)
-    blocks = jnp.stack([pairing, 2 * nc - 1 - pairing], axis=1).reshape(-1).astype(jnp.int32)
+    tokens_all = jnp.concatenate([flat(rows_mine[:, :count]), flat(rows_core[:, :count])], axis=0)
+    states_all = jnp.concatenate([flat(rows_mine[:, count:]), flat(rows_core[:, count:])], axis=0)
+    member = mine ^ jnp.array([2 * k + r for r in range(2) for k in range(chips)], dtype=jnp.int32)
+    match = member[:, None] == jnp.arange(nc, dtype=jnp.int32)[None, :]
+    paired = jnp.sum(jnp.where(match, pairing[None, :], 0), axis=1)
+    blocks = jnp.stack([paired, 2 * nc - 1 - paired], axis=1).reshape(-1).astype(jnp.int32)
+    own = blocks[:2]
 
     picks = (buckets[::-1][None, :] == jnp.arange(nbuckets, dtype=jnp.int32)[:, None]).astype(BF)
     bias = jnp.dot(table.T, picks, preferred_element_type=F32).reshape(pairs, 2, seq_len)
 
     rows_in = tokens[0].astype(F32)
-    incoming = cotangent[0]
-    a_one_full, norm_one_back = jax.vjp(norm_apply, rows_in, g_one)
-    a_one = a_one_full.astype(BF)
+    a_one, norm_one_back = jax.vjp(norm_apply, rows_in, g_one)
+    a_one = a_one.astype(BF)
     a_one_all = norm_apply(tokens_all.astype(F32), g_one).astype(BF)
     query = product(a_one, w_q).astype(BF)
     kv = product(a_one_all, w_kv).astype(BF)
+    attended, self_probs = self_forward(blocks, own, query, kv, bias)
+    attended, two_chips, three_z, incoming_chips = fence(attended, two_chips, three_z, incoming_chips)
+    two = net.join_chips(two, two_chips)
+    three = net.join_z(three, three_z)
+    two_core = net.to_core(two)
+    three_core = net.to_core(three)
+    incoming_rows = flat(jnp.stack((incoming,) + incoming_chips))
+    two = flat(net.join_cores(two, two_core))
+    w_o = two[:, :width]
+    c_q = two[:, width : 2 * width]
+    c_kv = two[:, 2 * width : 4 * width]
+    c_o = two[:, 4 * width :]
+    second = rows_in + product(attended, w_o)
     cross_kv = product(states_all, c_kv).astype(BF)
-    attended, self_probs = self_forward(blocks, own, query, kv, bias)
-    second = rows_in + product(attended, w_o)
     a_two, norm_two_back = jax.vjp(norm_apply, second, g_two)
     a_two = a_two.astype(BF)
     cross_q = product(a_two, c_q).astype(BF)
@@ -443,71 +563,142 @@
     third = second + product(cross_o, c_o)
     a_three, norm_three_back = jax.vjp(norm_apply, third, g_three)
     a_three = a_three.astype(BF)
-    gate = product(a_three, w_gate)
-    up_val = product(a_three, w_up)
-    hidden, geglu_back = jax.vjp(lambda left, right: jax.nn.gelu(left, approximate=True) * right, gate, up_val)
+
+    a_three_chips = net.spread_chips(a_three)
+    even = net.core == 0
+    three_low, three_high = jnp.where(even, three, three_core), jnp.where(even, three_core, three)
+    w_gu = jnp.stack([three_low[:, :half], three_high[:, :half]], axis=1)[..., : 2 * nz * wide].reshape(nz * shard, -1)
+    w_down = flat(jnp.stack([three_low[:, half:], three_high[:, half:]], axis=1)[..., :width])
+    w_gu, w_down, incoming_rows, a_three_chips = fence(w_gu, w_down, incoming_rows, a_three_chips)
+    a_three_rows = flat(jnp.stack((a_three,) + a_three_chips))
+    gate_up = product(a_three_rows, w_gu)
+    units = nz * wide
+    hidden, geglu_back = jax.vjp(
+        lambda left, right: jax.nn.gelu(left, approximate=True) * right, gate_up[:, :units], gate_up[:, units:]
+    )
     hidden = hidden.astype(BF)
-    result = third + product(hidden, w_down)
-
-    grad_hidden = through(incoming, w_down)
-    grad_down = weight_grad(hidden, incoming)
-    grad_gate, grad_up = geglu_back(grad_hidden)
-    grad_gate = grad_gate.astype(BF)
-    grad_up = grad_up.astype(BF)
-    grad_w_gate = weight_grad(a_three, grad_gate).astype(BF)
-    grad_w_up = weight_grad(a_three, grad_up).astype(BF)
-    total_down = net.reduce_weights(grad_down.astype(BF)).astype(F32)
-    total_ff = net.reduce_weights(jnp.concatenate([grad_w_gate, grad_w_up], axis=1)).astype(F32)
-    grad_a_three = through(grad_gate, w_gate) + through(grad_up, w_up)
-    part_three, grad_g_three = norm_three_back(grad_a_three)
+    grad_gate, grad_up = geglu_back(through(incoming_rows, w_down))
+    grad_gate_up = jnp.concatenate([grad_gate.astype(BF), grad_up.astype(BF)], axis=1)
+    grad_three_part = through(grad_gate_up, w_gu).astype(BF).reshape(chips, count, width)
+    result_part = product(hidden, w_down).astype(BF).reshape(chips, count, width)
+    grad_three_terms = net.swap_blocks(grad_three_part)
+    three_keep, three_give = split_grads(
+        net.core,
+        [(a_three_rows, grad_gate_up), (hidden, incoming_rows)],
+        [(half, 0, 0), (down_half, half, 0)],
+        pack_rows,
+        pack_cols,
+    )
+    grad_three_terms, three_keep, three_give, result_part = fence(
+        grad_three_terms, three_keep, three_give, result_part
+    )
+    three_core = net.to_core(three_give)
+    result_terms = net.swap_blocks(result_part)
+
+    part_three, grad_g_three = norm_three_back(net.add(grad_three_terms))
     grad_third = incoming.astype(F32) + part_three
     branch_two = grad_third.astype(BF)
-    grad_c_o = weight_grad(cross_o, branch_two)
     grad_cross_o = through(branch_two, c_o).astype(BF)
     dcq, dck, dcv = cross_backward(cross_q, cross_kv, grad_cross_o, cross_probs)
-    grad_c_q = weight_grad(a_two, dcq)
-    grad_c_k = weight_grad(states_all, dck)
-    grad_c_v = weight_grad(states_all, dcv)
+    dcq, dck, dcv, three_core, result_terms = fence(dcq, dck, dcv, three_core, result_terms)
+    result = third + net.add(result_terms)
+    three_terms = net.give_z(net.add((three_keep, three_core)).astype(BF))
     states_part = through(dck, c_kv[:, :width]) + through(dcv, c_kv[:, width:])
     part_two, grad_g_two = norm_two_back(through(dcq, c_q))
     grad_second = grad_third + part_two
     branch_one = grad_second.astype(BF)
-    grad_w_o = weight_grad(attended, branch_one)
-    total_two = net.reduce_weights(
-        jnp.concatenate([g.astype(BF) for g in (grad_w_o, grad_c_q, grad_c_k, grad_c_v, grad_c_o)], axis=1)
-    ).astype(F32)
+    two_keep, two_give = split_grads(
+        net.core,
+        [
+            (attended, branch_one),
+            (a_two, dcq),
+            (states_all, dck),
+            (states_all, dcv),
+            (cross_o, branch_two),
+        ],
+        [(each, 0, i * width) for i in range(5)],
+        each,
+        5 * width,
+    )
     grad_attended = through(branch_one, w_o).astype(BF)
+    grad_attended, two_keep, two_give, three_terms = fence(grad_attended, two_keep, two_give, three_terms)
+    two_keep = two_keep.reshape(nz, chips, each, -1)
+    two_core = net.to_core(two_give.reshape(nz, chips, each, -1))
+    three = net.add(three_terms).astype(BF)
+    three_chips = net.spread_chips(three)
     dq, dk, dv, bias_grad = self_backward(blocks, own, query, kv, grad_attended, self_probs)
+    dq, dk, dv, bias_grad, two_core, three_chips = fence(dq, dk, dv, bias_grad, two_core, three_chips)
+    three = jnp.stack((three,) + three_chips)
+    two_terms = net.give_chips(two_keep, two_core)
+    three_core = net.to_core(three)
+    rows_part = (through(dk, w_kv[:, :width]) + through(dv, w_kv[:, width:])).astype(BF).reshape(2, chips, count, width)
+    states_part = states_part.astype(BF).reshape(2, chips, -1, width)
+    sent_keep, sent_give = (jnp.concatenate([rows_part[r], states_part[r]], axis=1) for r in range(2))
+    sent_core = net.to_core(sent_give)
+    one_keep, one_give = split_grads(
+        net.core,
+        [(a_one, dq), (a_one_all, dk), (a_one_all, dv)],
+        [(each, 0, i * width) for i in range(3)],
+        each,
+        3 * width,
+    )
+    one_keep = one_keep.reshape(nz, chips, each, -1)
+    one_core = net.to_core(one_give.reshape(nz, chips, each, -1))
     table_grad = lax.dot_general(
         picks.astype(F32), bias_grad.reshape(heads, seq_len), LAST, precision=lax.Precision.HIGHEST
     )
-    grad_w_q = weight_grad(a_one, dq)
-    grad_w_k = weight_grad(a_one_all, dk)
-    grad_w_v = weight_grad(a_one_all, dv)
-    rows_part = through(dk, w_kv[:, :width]) + through(dv, w_kv[:, width:])
-    sent = jnp.concatenate(
-        [rows_part.astype(BF).reshape(nc, count, width), states_part.astype(BF).reshape(nc, -1, width)], axis=1
-    )
-    own_part = net.scatter_ctx(sent)
+    sent_core, one_core, two_terms, three_core, table_grad = fence(
+        sent_core, one_core, two_terms, three_core, table_grad
+    )
+    sent_terms = net.swap_blocks((sent_keep.astype(F32) + sent_core.astype(F32)).astype(BF))
+    one_terms = net.give_chips(one_keep, one_core)
+    two_terms = net.give_z(net.add(two_terms).astype(BF))
+    if wide % LANES == 0 and half % 16 == 0 and down_half % 16 == 0:
+        total_gate, total_up, total_down = place_ff(
+            net.chip, net.core, three, three_core, nz, half, wide, down_half, width
+        )
+    else:
+        joined = net.join_chips(three[:1], three[1:, None])
+        joined_other = net.join_chips(three_core[:1], three_core[1:, None])
+        joined = net.join_cores(joined, joined_other)[0].astype(F32)
+        total_gu = joined[:, :, :half, : 2 * units].reshape(chips, 2, half, 2, nz, wide)
+        total_gu = total_gu.transpose(3, 1, 2, 4, 0, 5).reshape(2, shard, -1)
+        total_gate, total_up = total_gu[0], total_gu[1]
+        total_down = joined[:, :, half:, :width].reshape(-1, width)
+    sent_terms, total_gate, total_up, total_down = fence(sent_terms, total_gate, total_up, total_down)
+    own_part = net.add(sent_terms)
     grad_a_one = through(dq, w_q) + own_part[:count]
     grad_states = own_part[count:]
     part_one, grad_g_one = norm_one_back(grad_a_one)
     grad_rows = grad_second + part_one
 
-    small_grad = jnp.stack([grad_g_one, grad_g_two, grad_g_three], axis=1).astype(BF)
-    small_grad = jnp.pad(small_grad, ((0, 0), (0, extra_width - 3)))
-    table_rows = jnp.pad(
-        table_grad.astype(BF).reshape(nz, 1, table_size),
-        ((0, 0), (0, shard - 1), (4, extra_width - 4 - table_size)),
-    ).reshape(nz * shard, extra_width)
-    total_one = net.reduce_weights(
-        jnp.concatenate(
-            [grad_w_q.astype(BF), grad_w_k.astype(BF), grad_w_v.astype(BF), small_grad + table_rows], axis=1
-        )
-    ).astype(F32)
-    small_total = total_one[:, 3 * width :]
-    gain_total = small_total[:, :4].T
-    table_total = small_total[0, 4 : 4 + table_size].reshape(-1, heads)
+    small_grad = jnp.pad(jnp.stack([grad_g_one, grad_g_two, grad_g_three]), ((0, 1), (0, 0)))
+    small_grad = small_grad.reshape(4, nz, shard).swapaxes(0, 1).reshape(nz, -1)
+    small_grad = jnp.concatenate([small_grad, table_grad.reshape(nz, table_size)], axis=1).astype(BF)
+    small_size = small_grad.shape[1]
+    small_cols = math.ceil(small_size / each)
+    small_width = LANES * math.ceil(small_cols / LANES)
+    small_grad = jnp.pad(small_grad, ((0, 0), (0, each * small_cols - small_size))).reshape(nz, each, small_cols)
+    small_grad = jnp.pad(small_grad, ((0, 0), (0, 0), (0, small_width - small_cols)))
+    one_terms, two_terms, small_grad = fence(one_terms, two_terms, small_grad)
+    one_sum = jnp.concatenate([net.add(one_terms).astype(BF), small_grad], axis=2)
+    one_terms = net.give_z(one_sum)
+    two = net.add(two_terms).astype(BF)[None]
+    two_chips = net.spread_chips(two)
+    one_terms, two_chips = fence(one_terms, two_chips)
+    one = net.add(one_terms).astype(BF)[None]
+    one_chips = net.spread_chips(one)
+    two = net.join_chips(two, two_chips)
+    two_core = net.to_core(two)
+    one_chips, two_core = fence(one_chips, two_core)
+    one = net.join_chips(one, one_chips)
+    one_core = net.to_core(one)
+    total_two = flat(net.join_cores(two, two_core)).astype(F32)
+    one = net.join_cores(one, one_core)
+    total_one = flat(one[..., : 3 * width]).astype(F32)
+    small_total = jnp.sum(one[..., 3 * width : 3 * width + small_cols].reshape(nc, -1).astype(F32), axis=0)
+    gain_total = small_total[: 4 * shard].reshape(4, shard)
+    table_total = small_total[4 * shard : 4 * shard + table_size].reshape(-1, heads)
 
     return (
         result.astype(BF)[None],
@@ -525,8 +716,8 @@
         total_two[:, 3 * width : 4 * width],
         total_two[:, 4 * width :],
         gain_total[2],
-        total_ff[:, :hidden_width],
-        total_ff[:, hidden_width:],
+        total_gate,
+        total_up,
         total_down,
     )
 

time: 551 us -> 389 us (0.71)
  waiting for transfers between devices: 258 us -> 119 us
  matrix products: 61.5 us -> 27 us
  starting transfers between devices: 61.9 us -> 89.9 us
  Pallas kernels: 29 us -> 57 us
  local copies, waits for them, and re-layouts: 84.1 us -> 57.6 us
  between operations: 16.9 us -> 1.99 us
    ppermute x36 -> x39, waiting for transfers between devices: 155 us -> 77.9 us  [to_chip(): return lax.ppermute(x, 'ctx', [(i, i ^ 2 * k) for i in range(self.nc)])]
    all_gather x3 -> x0, waiting for transfers between devices: 62.5 us -> none  [the longest x1 57.7 us: per_device(): lax.all_gather(rows_of(ff_down), ('fsdp', 'ctx'), axis=0, tiled=True)]
    dot_general x11 -> x0, matrix products: 22.6 us -> none  [weight_grad(): return lax.dot_general(a, grad, FIRST, preferred_element_type=F32)]
    ppermute x18, starting transfers between devices: 19.1 us -> 37.3 us  [along(): return lax.ppermute(x, 'fsdp', [(i, (i + s) % n) for i in range(n)])]
    pallas_call x0 -> x4, Pallas kernels: none -> 14.3 us  [the longest x3 11.1 us: split_grads(): pl.pallas_call(functools.partial(split_kernel, places, len(places)), in_s...]
    pallas_call x1, Pallas kernels: 4.67 us -> 18.6 us  [cross_backward(): pl.pallas_call(cross_backward_kernel, grid=(pairs,), in_specs=[column_blo...]
    concatenate x2 -> x1, local copies, waits for them, and re-layouts: 14.8 us -> 0.91 us  [per_device(): three = jnp.concatenate(columns_of(ff_gate) + columns_of(ff_up), axis=1)]
    ppermute x12 -> x11, starting transfers between devices: 9.09 us -> 19 us  [to_core(): return lax.ppermute(x, 'ctx', [(i, i ^ 1) for i in range(self.nc)])]
  transfers between devices with their start and end apart: 69 -> 68, of which waited for: 28 -> 23; matrix products, arithmetic and copies ran while one was open for 24% -> 21% of each run, Pallas kernels for 2% -> 13%
where the time goes in v2:
time: 389 us; the launch traced here: 387 us
  waiting for transfers between devices  119 us (31%)
  starting transfers between devices  89.9 us (23%)
  local copies, waits for them, and re-layouts  57.6 us (15%)
  Pallas kernels  57 us (15%)
  other arithmetic  33.6 us (9%)
  matrix products  27 us (7%)
    ppermute x39, waiting for transfers between devices, to_chip(): return lax.ppermute(x, 'ctx', [(i, i ^ 2 * k) for i in range(self.nc)])  77.9 us
    ppermute x18, waiting for transfers between devices, along(): return lax.ppermute(x, 'fsdp', [(i, (i + s) % n) for i in range(n)])  41.5 us
    ppermute x18, starting transfers between devices, along(): return lax.ppermute(x, 'fsdp', [(i, (i + s) % n) for i in range(n)])  37.3 us
    ppermute x39, starting transfers between devices, to_chip(): return lax.ppermute(x, 'ctx', [(i, i ^ 2 * k) for i in range(self.nc)])  33.6 us
    ppermute x11, starting transfers between devices, to_core(): return lax.ppermute(x, 'ctx', [(i, i ^ 1) for i in range(self.nc)])  19 us
    pallas_call x1, Pallas kernels, cross_backward(): pl.pallas_call(cross_backward_kernel, grid=(pairs,), in_specs=[column_blo...  18.6 us
    dot_general x10, matrix products, through(): return lax.dot_general(grad, w, LAST, preferred_element_type=F32)  17 us
    unnamed x88, local copies, waits for them, and re-layouts  12.8 us
  transfers between devices with their start and end apart: 68, of which 23 were waited for; matrix products, arithmetic and copies ran while one was open for 21% of the time, Pallas kernels for 13%

profile of v2, /device:TPU:1, one launch (start us, length us, event | category | flops | bytes accessed | tf_op | source)
XLA Modules:
  0.0 386.6 jit_solution(16767339263096972566)
XLA Ops:
  30.4 2.8 collective-permute-done.2
  37.6 3.1 collective-permute-start.11
  40.7 4.4 %collective-permute-start.9 = (bf16[4,192,768]{2,1,0:T(8,128)(2,1)S(1)}, bf16[4,192,768]{2,1,0:T(8,128)(2,1)S(1)}, u32[]{:S(2)}, u32[]{:S(2)}) collective-permute-start(bf16[4,192,768]{2,1,0:T(8,128)(2,1)S(1)} %pad_maximum_fusion.6), channel_id=1, source_target_pairs={{0,4},{4,0},{8,12},{12,8},{16,20},{20,16},{24,28},{28,24},{1,5},{5... | collective-permute-start | bytes 3538952 | tf_op jit(solution)/shard_map/ppermute | solution.py:375
  48.0 5.6 %collective-permute-done.11 = bf16[24,3840]{1,0:T(8,128)(2,1)S(1)} collective-permute-done((bf16[24,3840]{1,0:T(8,128)(2,1)}, bf16[24,3840]{1,0:T(8,128)(2,1)S(1)}, u32[]{:S(2)}, u32[]{:S(2)}) %collective-permute-start.11) | collective-permute-done | bytes 184352 | tf_op jit(solution)/shard_map/ppermute | solution.py:382
  53.8 5.3 %collective-permute-done.12 = bf16[24,3840]{1,0:T(8,128)(2,1)S(1)} collective-permute-done((bf16[24,3840]{1,0:T(8,128)(2,1)}, bf16[24,3840]{1,0:T(8,128)(2,1)S(1)}, u32[]{:S(2)}, u32[]{:S(2)}) %collective-permute-start.12) | collective-permute-done | bytes 184352 | tf_op jit(solution)/shard_map/ppermute | solution.py:382
  78.9 4.0 %convolution_convert_fusion.k_ref.v_ref = bf16[1024,1536]{1,0:T(8,128)(2,1)} fusion(bf16[1024,768]{1,0:T(8,128)(2,1)S(1)} %fusion.2.refs_2_.refs_4_, bf16[768,2432]{1,0:T(8,128)(2,1)S(1)} %bitcast.283), kind=kOutput, calls=%fused_computation.3 | convolution fusion | flops 2417491968 | bytes 7077888 | tf_op jit(solution)/shard_map/dot_general | solution.py:25
  83.2 21.0 %collective-permute-done.20 = bf16[128,768]{1,0:T(8,128)(2,1)} collective-permute-done((bf16[128,768]{1,0:T(8,128)(2,1)S(1)}, bf16[128,768]{1,0:T(8,128)(2,1)}, u32[]{:S(2)}, u32[]{:S(2)}) %collective-permute-start.20) | collective-permute-done | bytes 196640 | tf_op jit(solution)/shard_map/ppermute | solution.py:378
  104.8 5.0 %collective-permute-done.21 = bf16[128,768]{1,0:T(8,128)(2,1)S(1)} collective-permute-done((bf16[128,768]{1,0:T(8,128)(2,1)S(1)}, bf16[128,768]{1,0:T(8,128)(2,1)S(1)}, u32[]{:S(2)}, u32[]{:S(2)}) %collective-permute-start.21) | collective-permute-done | bytes 196640 | tf_op jit(solution)/shard_map/ppermute | solution.py:378
  110.4 4.9 %collective-permute-done.22 = bf16[128,768]{1,0:T(8,128)(2,1)S(1)} collective-permute-done((bf16[128,768]{1,0:T(8,128)(2,1)S(1)}, bf16[128,768]{1,0:T(8,128)(2,1)S(1)}, u32[]{:S(2)}, u32[]{:S(2)}) %collective-permute-start.22) | collective-permute-done | bytes 196640 | tf_op jit(solution)/shard_map/ppermute | solution.py:378
  119.4 9.4 %self_forward.1 = (bf16[128,768]{1,0:T(8,128)(2,1)S(1)}, bf16[6,256,1024]{2,1,0:T(8,128)(2,1)S(1)}) custom-call(s32[16]{0:T(128)S(1)} %reshape.269.blocks_ref, s32[2]{0:T(128)S(1)} %slice_reduce_fusion.3.own_ref, bf16[128,768]{1,0:T(8,128)(2,1)S(1)} %convolution_convert_fusion.7.q_ref, bf16[1024,1536]{1,0:T(8,128)(2,1)} %convolution_convert_fusion.k_ref.v_ref, ...), custom_call_target="tpu_custom_call" | custom-call | flops 805306368 | bytes 9437184 | tf_op jit(solution)/shard_map/self_forward/pallas_call | solution.py:174
  128.8 3.9 %collective-permute-done.18 = bf16[160,1024]{1,0:T(8,128)(2,1)S(1)} collective-permute-done((bf16[160,1024]{1,0:T(8,128)(2,1)S(1)}, bf16[160,1024]{1,0:T(8,128)(2,1)S(1)}, u32[]{:S(2)}, u32[]{:S(2)}) %collective-permute-start.18) | collective-permute-done | bytes 327712 | tf_op jit(solution)/shard_map/ppermute | solution.py:382
  154.2 3.9 %cross_forward.1 = (bf16[128,768]{1,0:T(8,128)(2,1)S(1)}, bf16[6,256,512]{2,1,0:T(8,128)(2,1)S(1)}) custom-call(bf16[128,768]{1,0:T(8,128)(2,1)S(1)} %convolution_convert_fusion.6.q_ref, bf16[512,1536]{1,0:T(8,128)(2,1)S(1)} %convolution_convert_fusion.1.k_ref.v_ref, bf16[512,1536]{1,0:T(8,128)(2,1)S(1)} %convolution_convert_fusion.1.k_ref.v_ref), custom_call_target="tpu_custom_call" | custom-call | flops 402653184 | bytes 4718592 | tf_op jit(solution)/shard_map/cross_forward/pallas_call | solution.py:242
  161.5 3.2 collective-permute-done.25
  164.8 4.3 %collective-permute-done.27 = bf16[128,768]{1,0:T(8,128)(2,1)S(1)} collective-permute-done((bf16[128,768]{1,0:T(8,128)(2,1)S(1)}, bf16[128,768]{1,0:T(8,128)(2,1)S(1)}, u32[]{:S(2)}, u32[]{:S(2)}) %collective-permute-start.27) | collective-permute-done | bytes 196640 | tf_op jit(solution)/shard_map/ppermute | solution.py:378
  178.0 4.9 %collective-permute-done.30 = bf16[128,768]{1,0:T(8,128)(2,1)S(1)} collective-permute-done((bf16[128,768]{1,0:T(8,128)(2,1)S(1)}, bf16[128,768]{1,0:T(8,128)(2,1)S(1)}, u32[]{:S(2)}, u32[]{:S(2)}) %collective-permute-start.30) | collective-permute-done | bytes 196640 | tf_op jit(solution)/shard_map/ppermute | solution.py:378
  182.9 2.7 collective-permute-start.31
  191.3 18.6 %cross_backward.1 = (bf16[128,768]{1,0:T(8,128)(2,1)S(1)}, bf16[512,768]{1,0:T(8,128)(2,1)S(1)}, bf16[512,768]{1,0:T(8,128)(2,1)S(1)}) custom-call(bf16[128,768]{1,0:T(8,128)(2,1)S(1)} %convolution_convert_fusion.6.q_ref, bf16[512,1536]{1,0:T(8,128)(2,1)S(1)} %convolution_convert_fusion.1.k_ref.v_ref, ...), custom_call_target="tpu_custom_call" | custom-call | flops 1006632960 | bytes 4718592 | tf_op jit(solution)/shard_map/cross_backward/pallas_call | solution.py:261
  212.7 7.1 %collective-permute-start.35 = (bf16[160,1024]{1,0:T(8,128)(2,1)S(1)}, bf16[160,1024]{1,0:T(8,128)(2,1)S(1)}, u32[]{:S(2)}, u32[]{:S(2)}) collective-permute-start(bf16[160,1024]{1,0:T(8,128)(2,1)S(1)} %get-tuple-element.308), channel_id=1, source_target_pairs={{0,1},{1,2},{2,3},{3,0},{4,5},{5,6},{6,7},{7,4},{8,9},{9,10},{10,1... | collective-permute-start | bytes 983048 | tf_op jit(solution)/shard_map/ppermute | solution.py:382
  222.9 4.9 %split_grads.4 = (bf16[16,24,3840]{2,1,0:T(8,128)(2,1)}, bf16[16,24,3840]{2,1,0:T(8,128)(2,1)}) custom-call(s32[1]{0:T(128)} %bitcast.67.core_ref, bf16[128,768]{1,0:T(8,128)(2,1)S(1)} %get-tuple-element.162.refs_0_, bf16[128,768]{1,0:T(8,128)(2,1)S(1)} %get-tuple-element.275.refs_1_, bf16[128,768]{1,0:T(8,128)(2,1)S(1)} %multiply_convert_fusion.3.refs_2_, ...), custom_call_target="tpu_custom_call" | custom-call | flops 1660944384 | bytes 10223616 | tf_op jit(solution)/shard_map/split_grads/pallas_call | solution.py:309
  229.6 13.2 %collective-permute-done.36 = bf16[160,1024]{1,0:T(8,128)(2,1)S(1)} collective-permute-done((bf16[160,1024]{1,0:T(8,128)(2,1)S(1)}, bf16[160,1024]{1,0:T(8,128)(2,1)S(1)}, u32[]{:S(2)}, u32[]{:S(2)}) %collective-permute-start.36) | collective-permute-done | bytes 327712 | tf_op jit(solution)/shard_map/ppermute | solution.py:382
  251.3 10.9 %self_backward.1 = (bf16[128,768]{1,0:T(8,128)(2,1)S(1)}, bf16[1024,768]{1,0:T(8,128)(2,1)S(1)}, bf16[1024,768]{1,0:T(8,128)(2,1)S(1)}, f32[6,2,1024]{2,1,0:T(2,128)S(1)}) custom-call(s32[16]{0:T(128)S(1)} %reshape.269.blocks_ref, s32[2]{0:T(128)S(1)} %slice_reduce_fusion.3.own_ref, bf16[128,768]{1,0:T(8,128)(2,1)S(1)} %convolution_convert_fusion.7.q_ref, ...), custom_call_target="tpu_custom_call" | custom-call | flops 2013265920 | bytes 9437184 | tf_op jit(solution)/shard_map/self_backward/pallas_call | solution.py:202
  267.2 4.8 %split_grads.5 = (bf16[16,24,2304]{2,1,0:T(8,128)(2,1)}, bf16[16,24,2304]{2,1,0:T(8,128)(2,1)}) custom-call(s32[1]{0:T(128)} %bitcast.67.core_ref, bf16[128,768]{1,0:T(8,128)(2,1)S(1)} %fusion.38.refs_0_, bf16[128,768]{1,0:T(8,128)(2,1)S(1)} %get-tuple-element.213.refs_1_, bf16[1024,768]{1,0:T(8,128)(2,1)S(1)} %fusion.2.refs_2_.refs_4_, ...), custom_call_target="tpu_custom_call" | custom-call | flops 2566914048 | bytes 10223616 | tf_op jit(solution)/shard_map/split_grads/pallas_call | solution.py:309
  273.0 3.3 fusion.29
  282.9 11.7 %collective-permute-done.44 = bf16[4,24,3840]{2,1,0:T(8,128)(2,1)S(1)} collective-permute-done((bf16[4,24,3840]{2,1,0:T(8,128)(2,1)S(1)}, bf16[4,24,3840]{2,1,0:T(8,128)(2,1)S(1)}, u32[]{:S(2)}, u32[]{:S(2)}) %collective-permute-start.44) | collective-permute-done | bytes 737312 | tf_op jit(solution)/shard_map/ppermute | solution.py:378
  298.4 14.8 %collective-permute-done.46 = bf16[4,24,3840]{2,1,0:T(8,128)(2,1)} collective-permute-done((bf16[4,24,3840]{2,1,0:T(8,128)(2,1)}, bf16[4,24,3840]{2,1,0:T(8,128)(2,1)}, u32[]{:S(2)}, u32[]{:S(2)}) %collective-permute-start.46) | collective-permute-done | bytes 737312 | tf_op jit(solution)/shard_map/ppermute | solution.py:378
  318.7 2.6 fusion.36
  325.6 3.2 place_ff.1
  331.3 7.2 %collective-permute-start.54 = (bf16[24,3840]{1,0:T(8,128)(2,1)}, bf16[24,3840]{1,0:T(8,128)(2,1)S(1)}, u32[]{:S(2)}, u32[]{:S(2)}) collective-permute-start(bf16[24,3840]{1,0:T(8,128)(2,1)} %get-tuple-element.328), channel_id=1, source_target_pairs={{0,1},{1,2},{2,3},{3,0},{4,5},{5,6},{6,7},{7,4},{8,9},{9,10},{10,1... | collective-permute-start | bytes 552968 | tf_op jit(solution)/shard_map/ppermute | solution.py:382
  345.9 7.0 %collective-permute-done.55 = bf16[24,3840]{1,0:T(8,128)(2,1)S(1)} collective-permute-done((bf16[24,3840]{1,0:T(8,128)(2,1)}, bf16[24,3840]{1,0:T(8,128)(2,1)S(1)}, u32[]{:S(2)}, u32[]{:S(2)}) %collective-permute-start.55) | collective-permute-done | bytes 184352 | tf_op jit(solution)/shard_map/ppermute | solution.py:382
  354.4 3.5 collective-permute-start.57
  363.8 3.2 collective-permute-done.58
  367.6 5.1 %collective-permute-start.66 = (bf16[1,4,24,3840]{3,2,1,0:T(8,128)(2,1)S(1)}, bf16[1,4,24,3840]{3,2,1,0:T(8,128)(2,1)S(1)}, u32[]{:S(2)}, u32[]{:S(2)}) collective-permute-start(bf16[1,4,24,3840]{3,2,1,0:T(8,128)(2,1)S(1)} %bitcast_dynamic-update-slice_fusion.12), channel_id=1, source_target_pairs={{0,4},{4,0},{8,12},{12,8},{16,20},{20,16},{24,28},{28,24},{1,5},{5... | collective-permute-start | bytes 2211848 | tf_op jit(solution)/shard_map/ppermute | solution.py:375
  (374 shorter events, 175.1 us)
Async XLA Ops:
  5.9 22.6 %collective-permute-start = (bf16[24,2432]{1,0:T(8,128)(2,1)}, bf16[24,2432]{1,0:T(8,128)(2,1)S(1)}, u32[]{:S(2)}, u32[]{:S(2)}) collective-permute-start(bf16[24,2432]{1,0:T(8,128)(2,1)} %pad_maximum_fusion.15), channel_id=1, source_target_pairs={{0,1},{1,2},{2,3},{3,0},{4,5},{5,6},{6,7},{7,4},{8,9},{9,10},{10,1... | collective-permute-start | bytes 350216 | tf_op jit(solution)/shard_map/ppermute | solution.py:382
  8.1 22.3 %collective-permute-start.1 = (bf16[24,2432]{1,0:T(8,128)(2,1)}, bf16[24,2432]{1,0:T(8,128)(2,1)}, u32[]{:S(2)}, u32[]{:S(2)}) collective-permute-start(bf16[24,2432]{1,0:T(8,128)(2,1)} %pad_maximum_fusion.15), channel_id=1, source_target_pairs={{0,2},{1,3},{2,0},{3,1},{4,6},{5,7},{6,4},{7,5},{8,10},{9,11},{10,... | collective-permute-start | bytes 350216 | tf_op jit(solution)/shard_map/ppermute | solution.py:382
  11.4 21.7 %collective-permute-start.3 = (bf16[192,768]{1,0:T(8,128)(2,1)S(1)}, bf16[192,768]{1,0:T(8,128)(2,1)S(1)}, u32[]{:S(2)}, u32[]{:S(2)}) collective-permute-start(bf16[192,768]{1,0:T(8,128)(2,1)S(1)} %get-tuple-element.335), channel_id=1, source_target_pairs={{0,8},{4,12},{8,0},{12,4},{16,24},{20,28},{24,16},{28,20},{1,9},{5... | collective-permute-start | bytes 884744 | tf_op jit(solution)/shard_map/ppermute | solution.py:378
  12.7 20.5 %collective-permute-start.4 = (bf16[192,768]{1,0:T(8,128)(2,1)S(1)}, bf16[192,768]{1,0:T(8,128)(2,1)S(1)}, u32[]{:S(2)}, u32[]{:S(2)}) collective-permute-start(bf16[192,768]{1,0:T(8,128)(2,1)S(1)} %get-tuple-element.335), channel_id=1, source_target_pairs={{0,16},{4,20},{8,24},{12,28},{16,0},{20,4},{24,8},{28,12},{1,17},{... | collective-permute-start | bytes 884744 | tf_op jit(solution)/shard_map/ppermute | solution.py:378
  13.9 19.2 %collective-permute-start.5 = (bf16[192,768]{1,0:T(8,128)(2,1)S(1)}, bf16[192,768]{1,0:T(8,128)(2,1)S(1)}, u32[]{:S(2)}, u32[]{:S(2)}) collective-permute-start(bf16[192,768]{1,0:T(8,128)(2,1)S(1)} %get-tuple-element.335), channel_id=1, source_target_pairs={{0,24},{4,28},{8,16},{12,20},{16,8},{20,12},{24,0},{28,4},{1,25},{... | collective-permute-start | bytes 884744 | tf_op jit(solution)/shard_map/ppermute | solution.py:378
  35.2 24.0 %collective-permute-start.6 = (bf16[4,24,2432]{2,1,0:T(8,128)(2,1)S(1)}, bf16[4,24,2432]{2,1,0:T(8,128)(2,1)S(1)}, u32[]{:S(2)}, u32[]{:S(2)}) collective-permute-start(bf16[4,24,2432]{2,1,0:T(8,128)(2,1)S(1)} %bitcast_dynamic-update-slice_fusion.24), channel_id=1, source_target_pairs={{0,8},{4,12},{8,0},{12,4},{16,24},{20,28},{24,16},{28,20},{1,9},{5... | collective-permute-start | bytes 1400840 | tf_op jit(solution)/shard_map/ppermute | solution.py:378
  36.4 22.7 %collective-permute-start.7 = (bf16[4,24,2432]{2,1,0:T(8,128)(2,1)S(1)}, bf16[4,24,2432]{2,1,0:T(8,128)(2,1)S(1)}, u32[]{:S(2)}, u32[]{:S(2)}) collective-permute-start(bf16[4,24,2432]{2,1,0:T(8,128)(2,1)S(1)} %bitcast_dynamic-update-slice_fusion.24), channel_id=1, source_target_pairs={{0,16},{4,20},{8,24},{12,28},{16,0},{20,4},{24,8},{28,12},{1,17},{... | collective-permute-start | bytes 1400840 | tf_op jit(solution)/shard_map/ppermute | solution.py:378
  40.7 18.7 %collective-permute-start.9 = (bf16[4,192,768]{2,1,0:T(8,128)(2,1)S(1)}, bf16[4,192,768]{2,1,0:T(8,128)(2,1)S(1)}, u32[]{:S(2)}, u32[]{:S(2)}) collective-permute-start(bf16[4,192,768]{2,1,0:T(8,128)(2,1)S(1)} %pad_maximum_fusion.6), channel_id=1, source_target_pairs={{0,4},{4,0},{8,12},{12,8},{16,20},{20,16},{24,28},{28,24},{1,5},{5... | collective-permute-start | bytes 3538952 | tf_op jit(solution)/shard_map/ppermute | solution.py:375
  65.7 67.0 %collective-permute-start.14 = (bf16[4,24,3840]{2,1,0:T(8,128)(2,1)}, bf16[4,24,3840]{2,1,0:T(8,128)(2,1)}, u32[]{:S(2)}, u32[]{:S(2)}) collective-permute-start(bf16[4,24,3840]{2,1,0:T(8,128)(2,1)} %bitcast_dynamic-update-slice_fusion.16), channel_id=1, source_target_pairs={{0,8},{4,12},{8,0},{12,4},{16,24},{20,28},{24,16},{28,20},{1,9},{5... | collective-permute-start | bytes 2211848 | tf_op jit(solution)/shard_map/ppermute | solution.py:378
  66.2 66.6 %collective-permute-start.15 = (bf16[4,24,3840]{2,1,0:T(8,128)(2,1)}, bf16[4,24,3840]{2,1,0:T(8,128)(2,1)}, u32[]{:S(2)}, u32[]{:S(2)}) collective-permute-start(bf16[4,24,3840]{2,1,0:T(8,128)(2,1)} %bitcast_dynamic-update-slice_fusion.16), channel_id=1, source_target_pairs={{0,16},{4,20},{8,24},{12,28},{16,0},{20,4},{24,8},{28,12},{1,17},{... | collective-permute-start | bytes 2211848 | tf_op jit(solution)/shard_map/ppermute | solution.py:378
  66.4 66.3 %collective-permute-start.16 = (bf16[4,24,3840]{2,1,0:T(8,128)(2,1)}, bf16[4,24,3840]{2,1,0:T(8,128)(2,1)}, u32[]{:S(2)}, u32[]{:S(2)}) collective-permute-start(bf16[4,24,3840]{2,1,0:T(8,128)(2,1)} %bitcast_dynamic-update-slice_fusion.16), channel_id=1, source_target_pairs={{0,24},{4,28},{8,16},{12,20},{16,8},{20,12},{24,0},{28,4},{1,25},{... | collective-permute-start | bytes 2211848 | tf_op jit(solution)/shard_map/ppermute | solution.py:378
  68.5 46.8 %collective-permute-start.17 = (bf16[160,1024]{1,0:T(8,128)(2,1)S(1)}, bf16[160,1024]{1,0:T(8,128)(2,1)}, u32[]{:S(2)}, u32[]{:S(2)}) collective-permute-start(bf16[160,1024]{1,0:T(8,128)(2,1)S(1)} %fusion.46), channel_id=1, source_target_pairs={{0,1},{1,2},{2,3},{3,0},{4,5},{5,6},{6,7},{7,4},{8,9},{9,10},{10,1... | collective-permute-start | bytes 983048 | tf_op jit(solution)/shard_map/ppermute | solution.py:382
  75.1 29.1 %collective-permute-start.20 = (bf16[128,768]{1,0:T(8,128)(2,1)S(1)}, bf16[128,768]{1,0:T(8,128)(2,1)}, u32[]{:S(2)}, u32[]{:S(2)}) collective-permute-start(bf16[128,768]{1,0:T(8,128)(2,1)S(1)} %bitcast.305), channel_id=1, source_target_pairs={{0,8},{4,12},{8,0},{12,4},{16,24},{20,28},{24,16},{28,20},{1,9},{5... | collective-permute-start | bytes 589832 | tf_op jit(solution)/shard_map/ppermute | solution.py:378
  115.3 17.4 %collective-permute-start.18 = (bf16[160,1024]{1,0:T(8,128)(2,1)S(1)}, bf16[160,1024]{1,0:T(8,128)(2,1)S(1)}, u32[]{:S(2)}, u32[]{:S(2)}) collective-permute-start(bf16[160,1024]{1,0:T(8,128)(2,1)S(1)} %fusion.46), channel_id=1, source_target_pairs={{0,2},{1,3},{2,0},{3,1},{4,6},{5,7},{6,4},{7,5},{8,10},{9,11},{10,... | collective-permute-start | bytes 983048 | tf_op jit(solution)/shard_map/ppermute | solution.py:382
  115.3 17.4 %collective-permute-start.19 = (bf16[160,1024]{1,0:T(8,128)(2,1)S(1)}, bf16[160,1024]{1,0:T(8,128)(2,1)S(1)}, u32[]{:S(2)}, u32[]{:S(2)}) collective-permute-start(bf16[160,1024]{1,0:T(8,128)(2,1)S(1)} %fusion.46), channel_id=1, source_target_pairs={{0,3},{1,0},{2,1},{3,2},{4,7},{5,4},{6,5},{7,6},{8,11},{9,8},{10,9... | collective-permute-start | bytes 983048 | tf_op jit(solution)/shard_map/ppermute | solution.py:382
  182.9 27.0 %collective-permute-start.31 = (bf16[4,160,1024]{2,1,0:T(8,128)(2,1)S(1)}, bf16[4,160,1024]{2,1,0:T(8,128)(2,1)S(1)}, u32[]{:S(2)}, u32[]{:S(2)}) collective-permute-start(bf16[4,160,1024]{2,1,0:T(8,128)(2,1)S(1)} %get-tuple-element.189), channel_id=1, source_target_pairs={{0,4},{4,0},{8,12},{12,8},{16,20},{20,16},{24,28},{28,24},{1,5},{5... | collective-permute-start | bytes 3932168 | tf_op jit(solution)/shard_map/ppermute | solution.py:375
  186.4 23.5 %collective-permute-start.32 = (bf16[128,768]{1,0:T(8,128)(2,1)S(1)}, bf16[128,768]{1,0:T(8,128)(2,1)S(1)}, u32[]{:S(2)}, u32[]{:S(2)}) collective-permute-start(bf16[128,768]{1,0:T(8,128)(2,1)S(1)} %get-tuple-element.320), channel_id=1, source_target_pairs={{0,8},{4,12},{8,0},{12,4},{16,24},{20,28},{24,16},{28,20},{1,9},{5... | collective-permute-start | bytes 589832 | tf_op jit(solution)/shard_map/ppermute | solution.py:378
  186.7 23.2 %collective-permute-start.33 = (bf16[128,768]{1,0:T(8,128)(2,1)S(1)}, bf16[128,768]{1,0:T(8,128)(2,1)S(1)}, u32[]{:S(2)}, u32[]{:S(2)}) collective-permute-start(bf16[128,768]{1,0:T(8,128)(2,1)S(1)} %get-tuple-element.319), channel_id=1, source_target_pairs={{0,16},{4,20},{8,24},{12,28},{16,0},{20,4},{24,8},{28,12},{1,17},{... | collective-permute-start | bytes 589832 | tf_op jit(solution)/shard_map/ppermute | solution.py:378
  187.7 22.2 %collective-permute-start.34 = (bf16[128,768]{1,0:T(8,128)(2,1)S(1)}, bf16[128,768]{1,0:T(8,128)(2,1)S(1)}, u32[]{:S(2)}, u32[]{:S(2)}) collective-permute-start(bf16[128,768]{1,0:T(8,128)(2,1)S(1)} %get-tuple-element.318), channel_id=1, source_target_pairs={{0,24},{4,28},{8,16},{12,20},{16,8},{20,12},{24,0},{28,4},{1,25},{... | collective-permute-start | bytes 589832 | tf_op jit(solution)/shard_map/ppermute | solution.py:378
  219.9 22.9 %collective-permute-start.36 = (bf16[160,1024]{1,0:T(8,128)(2,1)S(1)}, bf16[160,1024]{1,0:T(8,128)(2,1)S(1)}, u32[]{:S(2)}, u32[]{:S(2)}) collective-permute-start(bf16[160,1024]{1,0:T(8,128)(2,1)S(1)} %get-tuple-element.307), channel_id=1, source_target_pairs={{0,2},{1,3},{2,0},{3,1},{4,6},{5,7},{6,4},{7,5},{8,10},{9,11},{10,... | collective-permute-start | bytes 983048 | tf_op jit(solution)/shard_map/ppermute | solution.py:382
  220.8 22.0 %collective-permute-start.37 = (bf16[160,1024]{1,0:T(8,128)(2,1)S(1)}, bf16[160,1024]{1,0:T(8,128)(2,1)S(1)}, u32[]{:S(2)}, u32[]{:S(2)}) collective-permute-start(bf16[160,1024]{1,0:T(8,128)(2,1)S(1)} %get-tuple-element.306), channel_id=1, source_target_pairs={{0,3},{1,0},{2,1},{3,2},{4,7},{5,4},{6,5},{7,6},{8,11},{9,8},{10,9... | collective-permute-start | bytes 983048 | tf_op jit(solution)/shard_map/ppermute | solution.py:382
  242.8 21.5 %collective-permute-start.38 = (bf16[4,4,24,3840]{3,2,1,0:T(8,128)(2,1)}, bf16[4,4,24,3840]{3,2,1,0:T(8,128)(2,1)}, u32[]{:S(2)}, u32[]{:S(2)}) collective-permute-start(bf16[4,4,24,3840]{3,2,1,0:T(8,128)(2,1)} %bitcast.334), channel_id=1, source_target_pairs={{0,4},{4,0},{8,12},{12,8},{16,20},{20,16},{24,28},{28,24},{1,5},{5... | collective-permute-start | bytes 8847368 | tf_op jit(solution)/shard_map/ppermute | solution.py:375
  272.0 41.2 %collective-permute-start.43 = (bf16[4,4,24,2304]{3,2,1,0:T(8,128)(2,1)}, bf16[4,4,24,2304]{3,2,1,0:T(8,128)(2,1)}, u32[]{:S(2)}, u32[]{:S(2)}) collective-permute-start(bf16[4,4,24,2304]{3,2,1,0:T(8,128)(2,1)} %bitcast.335), channel_id=1, source_target_pairs={{0,4},{4,0},{8,12},{12,8},{16,20},{20,16},{24,28},{28,24},{1,5},{5... | collective-permute-start | bytes 5308424 | tf_op jit(solution)/shard_map/ppermute | solution.py:375
  276.3 18.2 %collective-permute-start.44 = (bf16[4,24,3840]{2,1,0:T(8,128)(2,1)S(1)}, bf16[4,24,3840]{2,1,0:T(8,128)(2,1)S(1)}, u32[]{:S(2)}, u32[]{:S(2)}) collective-permute-start(bf16[4,24,3840]{2,1,0:T(8,128)(2,1)S(1)} %get-tuple-element.280), channel_id=1, source_target_pairs={{0,8},{4,12},{8,0},{12,4},{16,24},{20,28},{24,16},{28,20},{1,9},{5... | collective-permute-start | bytes 2211848 | tf_op jit(solution)/shard_map/ppermute | solution.py:378
  278.6 34.6 %collective-permute-start.47 = (bf16[4,160,1024]{2,1,0:T(8,128)(2,1)S(1)}, bf16[4,160,1024]{2,1,0:T(8,128)(2,1)S(1)}, u32[]{:S(2)}, u32[]{:S(2)}) collective-permute-start(bf16[4,160,1024]{2,1,0:T(8,128)(2,1)S(1)} %pad_maximum_fusion.5.own_ref), channel_id=1, source_target_pairs={{0,4},{4,0},{8,12},{12,8},{16,20},{20,16},{24,28},{28,24},{1,5},{5... | collective-permute-start | bytes 3932168 | tf_op jit(solution)/shard_map/ppermute | solution.py:375
  280.0 33.2 %collective-permute-start.42 = (bf16[4,192,768]{2,1,0:T(8,128)(2,1)}, bf16[4,192,768]{2,1,0:T(8,128)(2,1)}, u32[]{:S(2)}, u32[]{:S(2)}) collective-permute-start(bf16[4,192,768]{2,1,0:T(8,128)(2,1)} %pad_maximum_fusion.7), channel_id=1, source_target_pairs={{0,4},{4,0},{8,12},{12,8},{16,20},{20,16},{24,28},{28,24},{1,5},{5... | collective-permute-start | bytes 3538952 | tf_op jit(solution)/shard_map/ppermute | solution.py:375
  280.3 18.1 %collective-permute-start.45 = (bf16[4,24,3840]{2,1,0:T(8,128)(2,1)}, bf16[4,24,3840]{2,1,0:T(8,128)(2,1)}, u32[]{:S(2)}, u32[]{:S(2)}) collective-permute-start(bf16[4,24,3840]{2,1,0:T(8,128)(2,1)} %get-tuple-element.279), channel_id=1, source_target_pairs={{0,16},{4,20},{8,24},{12,28},{16,0},{20,4},{24,8},{28,12},{1,17},{... | collective-permute-start | bytes 2211848 | tf_op jit(solution)/shard_map/ppermute | solution.py:378
  294.6 18.7 %collective-permute-start.46 = (bf16[4,24,3840]{2,1,0:T(8,128)(2,1)}, bf16[4,24,3840]{2,1,0:T(8,128)(2,1)}, u32[]{:S(2)}, u32[]{:S(2)}) collective-permute-start(bf16[4,24,3840]{2,1,0:T(8,128)(2,1)} %fusion.30), channel_id=1, source_target_pairs={{0,24},{4,28},{8,16},{12,20},{16,8},{20,12},{24,0},{28,4},{1,25},{... | collective-permute-start | bytes 2211848 | tf_op jit(solution)/shard_map/ppermute | solution.py:378
  317.5 21.0 %collective-permute-start.50 = (bf16[192,768]{1,0:T(8,128)(2,1)}, bf16[192,768]{1,0:T(8,128)(2,1)}, u32[]{:S(2)}, u32[]{:S(2)}) collective-permute-start(bf16[192,768]{1,0:T(8,128)(2,1)} %get-tuple-element.310), channel_id=1, source_target_pairs={{0,24},{4,28},{8,16},{12,20},{16,8},{20,12},{24,0},{28,4},{1,25},{... | collective-permute-start | bytes 884744 | tf_op jit(solution)/shard_map/ppermute | solution.py:378
  321.3 31.6 %collective-permute-start.51 = (bf16[4,24,2304]{2,1,0:T(8,128)(2,1)}, bf16[4,24,2304]{2,1,0:T(8,128)(2,1)}, u32[]{:S(2)}, u32[]{:S(2)}) collective-permute-start(bf16[4,24,2304]{2,1,0:T(8,128)(2,1)} %get-tuple-element.287), channel_id=1, source_target_pairs={{0,8},{4,12},{8,0},{12,4},{16,24},{20,28},{24,16},{28,20},{1,9},{5... | collective-permute-start | bytes 1327112 | tf_op jit(solution)/shard_map/ppermute | solution.py:378
  322.4 30.5 %collective-permute-start.52 = (bf16[4,24,2304]{2,1,0:T(8,128)(2,1)}, bf16[4,24,2304]{2,1,0:T(8,128)(2,1)}, u32[]{:S(2)}, u32[]{:S(2)}) collective-permute-start(bf16[4,24,2304]{2,1,0:T(8,128)(2,1)} %get-tuple-element.286), channel_id=1, source_target_pairs={{0,16},{4,20},{8,24},{12,28},{16,0},{20,4},{24,8},{28,12},{1,17},{... | collective-permute-start | bytes 1327112 | tf_op jit(solution)/shard_map/ppermute | solution.py:378
  330.1 22.8 %collective-permute-start.53 = (bf16[4,24,2304]{2,1,0:T(8,128)(2,1)S(1)}, bf16[4,24,2304]{2,1,0:T(8,128)(2,1)S(1)}, u32[]{:S(2)}, u32[]{:S(2)}) collective-permute-start(bf16[4,24,2304]{2,1,0:T(8,128)(2,1)S(1)} %fusion.37), channel_id=1, source_target_pairs={{0,24},{4,28},{8,16},{12,20},{16,8},{20,12},{24,0},{28,4},{1,25},{... | collective-permute-start | bytes 1327112 | tf_op jit(solution)/shard_map/ppermute | solution.py:378
  (74 other events, 654.7 us)
